TPU v7x, 32 devices: a whole 2x2x4 slice. The times are simulated.
32 devices in a mesh: fsdp: 16 (over z, x, core), seq: 2 (over y).
Axes of the slice: x: 2, y: 2, z: 4, core: 2. Of those that a mesh axis runs over, the one named last changes fastest.
Arguments:
- inputs: bfloat16 [64, 512, 768], P('fsdp', 'seq'), may hold values from -6 to 6
- segment_ids: int32 [64, 512], P('fsdp'), may hold values from 0 to 7, as said below
- token_flags: int32 [64, 512], P('fsdp'), may hold values from 0 to 1, as said below
- output_grad: bfloat16 [64, 512, 768], P('fsdp', 'seq'), may hold values from -6 to 6
- attention_weights: float32 [768, 3072], P(None, ('fsdp', 'seq'))
- feedforward_weights: float32 [768, 6144], P(None, ('fsdp', 'seq')), may hold values from -0.21875 to 0.21875
- layer_vectors: float32 [3, 3072], P(None, ('fsdp', 'seq'))
- attention_first: float32 [768, 3072], P(None, ('fsdp', 'seq')), may hold values from -512 to 512
- attention_second: float32 [768, 3072], P(None, ('fsdp', 'seq')), may hold values from 4096 to 65536
- feedforward_first: float32 [768, 6144], P(None, ('fsdp', 'seq')), may hold values from -512 to 512
- feedforward_second: float32 [768, 6144], P(None, ('fsdp', 'seq')), may hold values from 4096 to 65536
- vector_first: float32 [3, 3072], P(None, ('fsdp', 'seq')), may hold values from -1024 to 1024
- vector_second: float32 [3, 3072], P(None, ('fsdp', 'seq')), may hold values from 16384 to 262144
Outputs:
- layer_output: bfloat16 [64, 512, 768], P('fsdp', 'seq')
- input_grad: bfloat16 [64, 512, 768], P('fsdp', 'seq')
- pooled: float32 [64, 8, 768], P('fsdp', None, 'seq')
- stream_rms: float32 [3], replicated
- attention_new: float32 [768, 3072], P(None, ('fsdp', 'seq'))
- attention_first_new: float32 [768, 3072], P(None, ('fsdp', 'seq'))
- attention_second_new: float32 [768, 3072], P(None, ('fsdp', 'seq'))
- attention_low: bfloat16 [768, 3072], P(None, ('fsdp', 'seq'))
- feedforward_new: float32 [768, 6144], P(None, ('fsdp', 'seq'))
- feedforward_first_new: float32 [768, 6144], P(None, ('fsdp', 'seq'))
- feedforward_second_new: float32 [768, 6144], P(None, ('fsdp', 'seq'))
- feedforward_low: bfloat16 [768, 6144], P(None, ('fsdp', 'seq'))
- vectors_new: float32 [3, 3072], P(None, ('fsdp', 'seq'))
- vector_first_new: float32 [3, 3072], P(None, ('fsdp', 'seq'))
- vector_second_new: float32 [3, 3072], P(None, ('fsdp', 'seq'))
- vectors_low: bfloat16 [3, 3072], P(None, ('fsdp', 'seq'))
Inputs may be any that keep to these rules, and one draw needn't show every extreme that they name: `segment_ids`: within each row the ids never fall and every id from 0 to 7 occurs. `token_flags`: the first position of every row is 1.
All inputs are finite; a program needn't handle non-finite values.
Results may differ from a plain program's by a relative error of at most 0.015.
Values may be sent and summed in bfloat16 or wider, within the bound.
A program may use at most 192 MiB of HBM per device.

v0:
```python
import functools
import math
import types

import jax
import jax.numpy as jnp
from jax import lax
from jax.experimental import pallas as pl
from jax.experimental.pallas import tpu as pltpu
from jax.sharding import PartitionSpec as P

D = 768
HEADS = 12
HEAD_DIM = 64
FF = 3072
SEGMENTS = 8
STEP = 5


norm_epsilon = 1e-12
adam_epsilon = 1e-08
beta_first = 0.5
beta_second = 0.5
weight_decay = 0.01
rate_attention = 0.04
rate_feedforward = 0.03
rate_vectors = 0.2
masked_score = -1e30


def plain_dot(left_side, right_side):
    return jnp.dot(left_side, right_side, preferred_element_type=jnp.float32)


def contract_rows(left_side, right_side):
    return lax.dot_general(
        left_side, right_side, (((0,), (0,)), ((), ())), preferred_element_type=jnp.float32
    )


def contract_columns(left_side, right_side):
    return lax.dot_general(
        left_side, right_side, (((1,), (1,)), ((), ())), preferred_element_type=jnp.float32
    )


def normalize(stream):
    average = jnp.mean(stream, axis=-1, keepdims=True)
    centered = stream - average
    variance = jnp.mean(centered * centered, axis=-1, keepdims=True)
    inverse = lax.rsqrt(variance + norm_epsilon)
    return (centered * inverse, inverse)


def norm_back(grad_normed, normed, inverse):
    return inverse * (
        grad_normed
        - jnp.mean(grad_normed, axis=-1, keepdims=True)
        - normed * jnp.mean(grad_normed * normed, axis=-1, keepdims=True)
    )


def gelu_slope(value):
    return 0.5 * (1.0 + lax.erf(value * math.sqrt(0.5))) + value * jnp.exp(
        -0.5 * value * value
    ) / math.sqrt(2.0 * math.pi)


def masked_scores(queries, key_part, query_ids, key_ids):
    scores = jnp.einsum("rqhd,rkhd->rhqk", queries, key_part, preferred_element_type=jnp.float32)
    same_segment = query_ids[:, None, :, None] == key_ids[:, None, None, :]
    return jnp.where(same_segment, scores, masked_score)


def attend_block(pieces):
    queries, key_part, value_part, query_ids, key_ids = pieces
    scores = masked_scores(queries, key_part, query_ids, key_ids)
    largest = jnp.max(scores, axis=-1, keepdims=True)
    exponent = jnp.exp(scores - largest)
    denominator = jnp.sum(exponent, axis=-1, keepdims=True)
    soft_weights = (exponent / denominator).astype(jnp.bfloat16)
    context = jnp.einsum(
        "rhqk,rkhd->rqhd", soft_weights, value_part, preferred_element_type=jnp.float32
    )
    return (context, (largest + jnp.log(denominator))[..., 0])


def attend_back(pieces):
    queries, key_part, value_part, query_ids, key_ids, log_total, grad_context = pieces
    scores = masked_scores(queries, key_part, query_ids, key_ids)
    soft_again = jnp.exp(scores - log_total[..., None])
    grad_soft = jnp.einsum(
        "rqhd,rkhd->rhqk", grad_context, value_part, preferred_element_type=jnp.float32
    )
    inner_sum = jnp.sum(soft_again * grad_soft, axis=-1, keepdims=True)
    grad_scores = (soft_again * (grad_soft - inner_sum)).astype(jnp.bfloat16)
    grad_queries = jnp.einsum(
        "rhqk,rkhd->rqhd", grad_scores, key_part, preferred_element_type=jnp.float32
    )
    grad_keys = jnp.einsum(
        "rhqk,rqhd->rkhd", grad_scores, queries, preferred_element_type=jnp.float32
    )
    grad_values = jnp.einsum(
        "rhqk,rqhd->rkhd",
        soft_again.astype(jnp.bfloat16),
        grad_context,
        preferred_element_type=jnp.float32,
    )
    return (grad_queries, grad_keys, grad_values)


def adamw_update(weight, gradient, first_moment, second_moment, step_rate, decay_rate):
    first_new = beta_first * first_moment + (1.0 - beta_first) * gradient
    second_new = beta_second * second_moment + (1.0 - beta_second) * gradient * gradient
    correction_first = 1.0 - beta_first**STEP
    correction_second = 1.0 - beta_second**STEP
    update = (
        first_new / correction_first / (jnp.sqrt(second_new / correction_second) + adam_epsilon)
    )
    weight_new = weight - step_rate * (update + decay_rate * weight)
    return (weight_new, first_new, second_new, weight_new.astype(jnp.bfloat16))


def plain_shards(
    inputs,
    segment_ids,
    token_flags,
    output_grad,
    attention_weights,
    feedforward_weights,
    layer_vectors,
    attention_first,
    attention_second,
    feedforward_first,
    feedforward_second,
    vector_first,
    vector_second,
):
    row_count, local_span, model_width = inputs.shape
    full_length = segment_ids.shape[1]
    score_scale = HEAD_DIM ** (-0.5)
    inputs_here, grad_here = (inputs, output_grad)
    offset = lax.axis_index("seq") * local_span
    query_ids = lax.dynamic_slice_in_dim(segment_ids, offset, local_span, 1)
    work_flags = lax.dynamic_slice_in_dim(token_flags, offset, local_span, 1).astype(jnp.float32)
    work_span = inputs_here.shape[1]
    attention_full, feedforward_full, vector_low = (
        lax.all_gather(attention_weights.astype(jnp.bfloat16), ("fsdp", "seq"), axis=1, tiled=True),
        lax.all_gather(
            feedforward_weights.astype(jnp.bfloat16), ("fsdp", "seq"), axis=1, tiled=True
        ),
        lax.all_gather(layer_vectors.astype(jnp.bfloat16), ("fsdp", "seq"), axis=1, tiled=True),
    )
    vector_wide = vector_low.astype(jnp.float32)
    tokens = inputs_here.reshape(-1, D)
    tokens_wide = tokens.astype(jnp.float32)
    projected = plain_dot(tokens, attention_full[:, : 3 * D])
    queries = ((projected[:, :D] + vector_wide[0, :D]) * score_scale).astype(jnp.bfloat16)
    key_part = projected[:, D : 2 * D].astype(jnp.bfloat16)
    value_part = (projected[:, 2 * D :] + vector_wide[0, D : 2 * D]).astype(jnp.bfloat16)
    key_rows, value_rows = (
        lax.all_gather(key_part.reshape(row_count, work_span, D), "seq", axis=1, tiled=True),
        lax.all_gather(value_part.reshape(row_count, work_span, D), "seq", axis=1, tiled=True),
    )
    group_rows = math.gcd(row_count, max(1, 512 // work_span))
    block_count = row_count // group_rows
    query_blocks = queries.reshape(block_count, group_rows, work_span, HEADS, HEAD_DIM)
    key_blocks = key_rows.reshape(block_count, group_rows, full_length, HEADS, HEAD_DIM)
    value_blocks = value_rows.reshape(block_count, group_rows, full_length, HEADS, HEAD_DIM)
    query_id_blocks = query_ids.reshape(block_count, group_rows, work_span)
    key_id_blocks = segment_ids.reshape(block_count, group_rows, full_length)
    context, log_total = lax.map(
        attend_block, (query_blocks, key_blocks, value_blocks, query_id_blocks, key_id_blocks)
    )
    context_low = context.reshape(-1, D).astype(jnp.bfloat16)
    attention_out = (
        plain_dot(context_low, attention_full[:, 3 * D :]) + vector_wide[0, 2 * D : 3 * D]
    )
    first_normed, first_inverse = normalize(tokens_wide + attention_out)
    first_norm = (first_normed * vector_wide[2, :D] + vector_wide[2, D : 2 * D]).astype(
        jnp.bfloat16
    )
    up_value = plain_dot(first_norm, feedforward_full[:, :FF]) + vector_wide[1]
    activated = jax.nn.gelu(up_value, approximate=False).astype(jnp.bfloat16)
    feed_out = contract_columns(activated, feedforward_full[:, FF:]) + vector_wide[0, 3 * D :]
    second_normed, second_inverse = normalize(first_norm.astype(jnp.float32) + feed_out)
    layer_output = (second_normed * vector_wide[2, 2 * D : 3 * D] + vector_wide[2, 3 * D :]).astype(
        jnp.bfloat16
    )
    output_rows = layer_output.reshape(row_count, work_span, D)
    flat_flags = work_flags.reshape(-1)
    squares = jnp.stack(
        [
            jnp.sum(flat_flags * jnp.mean(tokens_wide * tokens_wide, axis=-1)),
            jnp.sum(flat_flags * jnp.mean(attention_out * attention_out, axis=-1)),
            jnp.sum(flat_flags * jnp.mean(feed_out * feed_out, axis=-1)),
        ]
    )
    square_total, flag_total = lax.psum((squares, jnp.sum(flat_flags)), ("fsdp", "seq"))
    stream_rms = jnp.sqrt(square_total / flag_total)
    segment_range = jnp.arange(SEGMENTS, dtype=jnp.int32)
    members = (query_ids[:, None, :] == segment_range[None, :, None]).astype(
        jnp.float32
    ) * work_flags[:, None, :]
    partial_pool = jnp.einsum(
        "rsl,rld->rsd",
        members.astype(jnp.bfloat16),
        output_rows,
        preferred_element_type=jnp.float32,
    )
    pool_share = lax.psum_scatter(
        partial_pool.astype(jnp.bfloat16), "seq", scatter_dimension=2, tiled=True
    ).astype(jnp.float32)
    full_members = (segment_ids[:, None, :] == segment_range[None, :, None]).astype(jnp.float32)
    full_members = full_members * token_flags[:, None, :].astype(jnp.float32)
    counts = jnp.sum(full_members, axis=2)
    pooled = pool_share / jnp.maximum(counts, 1.0)[:, :, None]
    attention_back, feedforward_back, vector_again = (
        lax.all_gather(attention_weights.astype(jnp.bfloat16), ("fsdp", "seq"), axis=1, tiled=True),
        lax.all_gather(
            feedforward_weights.astype(jnp.bfloat16), ("fsdp", "seq"), axis=1, tiled=True
        ),
        lax.all_gather(layer_vectors.astype(jnp.bfloat16), ("fsdp", "seq"), axis=1, tiled=True),
    )
    vector_back = vector_again.astype(jnp.float32)
    grad_out = grad_here.reshape(-1, D).astype(jnp.float32)
    grad_gain_second = jnp.sum(grad_out * second_normed, axis=0)
    grad_shift_second = jnp.sum(grad_out, axis=0)
    grad_second = norm_back(grad_out * vector_back[2, 2 * D : 3 * D], second_normed, second_inverse)
    grad_feed = grad_second.astype(jnp.bfloat16)
    grad_bias_down = jnp.sum(grad_feed.astype(jnp.float32), axis=0)
    grad_down = contract_rows(grad_feed, activated)
    grad_activated = plain_dot(grad_feed, feedforward_back[:, FF:])
    grad_up = (grad_activated * gelu_slope(up_value)).astype(jnp.bfloat16)
    grad_bias_up = jnp.sum(grad_up.astype(jnp.float32), axis=0)
    grad_up_weight = contract_rows(first_norm, grad_up)
    grad_first = grad_second + contract_columns(grad_up, feedforward_back[:, :FF])
    grad_feedforward = jnp.concatenate([grad_up_weight, grad_down], axis=1)
    grad_gain_first = jnp.sum(grad_first * first_normed, axis=0)
    grad_shift_first = jnp.sum(grad_first, axis=0)
    grad_stream = norm_back(grad_first * vector_back[2, :D], first_normed, first_inverse)
    grad_attention_out = grad_stream.astype(jnp.bfloat16)
    grad_bias_out = jnp.sum(grad_attention_out.astype(jnp.float32), axis=0)
    grad_out_weight = contract_rows(context_low, grad_attention_out)
    grad_context = contract_columns(grad_attention_out, attention_back[:, 3 * D :]).astype(
        jnp.bfloat16
    )
    grad_query, grad_key_rows, grad_value_rows = lax.map(
        attend_back,
        (
            query_blocks,
            key_blocks,
            value_blocks,
            query_id_blocks,
            key_id_blocks,
            log_total,
            grad_context.reshape(block_count, group_rows, work_span, HEADS, HEAD_DIM),
        ),
    )
    key_share, value_share = (
        lax.psum_scatter(
            grad_key_rows.reshape(row_count, full_length, D).astype(jnp.bfloat16),
            "seq",
            scatter_dimension=1,
            tiled=True,
        ).astype(jnp.float32),
        lax.psum_scatter(
            grad_value_rows.reshape(row_count, full_length, D).astype(jnp.bfloat16),
            "seq",
            scatter_dimension=1,
            tiled=True,
        ).astype(jnp.float32),
    )
    grad_query_low = grad_query.reshape(-1, D).astype(jnp.bfloat16) * score_scale
    grad_key_low = key_share.reshape(-1, D).astype(jnp.bfloat16)
    grad_value_low = value_share.reshape(-1, D).astype(jnp.bfloat16)
    grad_projected = jnp.concatenate([grad_query_low, grad_key_low, grad_value_low], axis=1)
    grad_bias_query = jnp.sum(grad_query_low.astype(jnp.float32), axis=0)
    grad_bias_value = jnp.sum(grad_value_low.astype(jnp.float32), axis=0)
    grad_in_weight = contract_rows(tokens, grad_projected)
    input_rows = (
        grad_stream + contract_columns(grad_projected, attention_back[:, : 3 * D])
    ).astype(jnp.bfloat16)
    input_rows = input_rows.reshape(row_count, work_span, D)
    grad_attention = jnp.concatenate([grad_in_weight, grad_out_weight], axis=1)
    grad_vectors = jnp.stack(
        [
            jnp.concatenate([grad_bias_query, grad_bias_value, grad_bias_out, grad_bias_down]),
            grad_bias_up,
            jnp.concatenate(
                [grad_gain_first, grad_shift_first, grad_gain_second, grad_shift_second]
            ),
        ]
    )
    attention_share, feedforward_share, vector_share = (
        lax.psum_scatter(grad_attention, ("fsdp", "seq"), scatter_dimension=1, tiled=True),
        lax.psum_scatter(grad_feedforward, ("fsdp", "seq"), scatter_dimension=1, tiled=True),
        lax.psum_scatter(grad_vectors, ("fsdp", "seq"), scatter_dimension=1, tiled=True),
    )
    attention_new, attention_first_new, attention_second_new, attention_low = adamw_update(
        attention_weights,
        attention_share,
        attention_first,
        attention_second,
        rate_attention,
        weight_decay,
    )
    feedforward_new, feedforward_first_new, feedforward_second_new, feedforward_low = adamw_update(
        feedforward_weights,
        feedforward_share,
        feedforward_first,
        feedforward_second,
        rate_feedforward,
        weight_decay,
    )
    vectors_new, vector_first_new, vector_second_new, vectors_low = adamw_update(
        layer_vectors, vector_share, vector_first, vector_second, rate_vectors, 0.0
    )
    return (
        output_rows,
        input_rows,
        pooled,
        stream_rms,
        attention_new,
        attention_first_new,
        attention_second_new,
        attention_low,
        feedforward_new,
        feedforward_first_new,
        feedforward_second_new,
        feedforward_low,
        vectors_new,
        vector_first_new,
        vector_second_new,
        vectors_low,
    )


MESH = pl.DeviceIdType.MESH
F32 = jnp.float32
BF16 = jnp.bfloat16

NZ, NX, NC, NY = 4, 2, 2, 2
ROW = 512
OWN_ROWS = 2
TOKENS = OWN_ROWS * ROW
SHARD_A = 96
SHARD_F = 192
EXTRA = 16
FULL_A = SHARD_A + EXTRA
PIECES = 3
PIECE = SHARD_F // PIECES
BLOCK = FF // PIECES
SPLIT_F = 48


def tn_dot(left_side, right_side):
    return contract_rows(left_side, right_side)


def nt_dot(left_side, right_side):
    return contract_columns(left_side, right_side)


def column_sum(value):
    return jnp.sum(value, axis=0, keepdims=True)


def row_mean(value):
    return jnp.mean(value, axis=-1, keepdims=True)


def remote(src, dst, send, recv, where):
    return pltpu.make_async_remote_copy(
        src_ref=src,
        dst_ref=dst,
        send_sem=send,
        recv_sem=recv,
        device_id=where,
        device_id_type=MESH,
    )


PLAN = (
    (0, 15, 30, 45), (), (16, 260), (1,),
    (
        17, 18, 23, 46, 60, 75, 2, 3, 8, 31, 19, 20, 261, 47, 48, 9, 4, 5,
        24, 32, 33, 25, 90, 105, 10, 21, 22, 53, 49, 50, 76, 38, 26, 27, 6, 7,
        34, 35, 61, 11, 12, 51, 52, 77, 78, 39, 40, 13, 14, 36, 37, 41, 42, 54,
        55, 62, 63, 28, 29, 120, 135, 68, 79, 80, 106, 56, 57, 43, 44, 83, 58, 59,
        64, 65, 91,
    ),
    (81, 82, 84, 85, 86, 87, 107, 108), (), (66, 67, 69, 70, 88, 89, 113),
    (71, 72, 92, 93, 114, 115), (98, 109, 110, 136), (73, 74, 262),
    (94, 95, 111, 112, 99, 117, 116, 121, 138, 137, 143), (100,), (96, 97, 263), (101, 102),
    (122, 123), (128, 139, 140), (103, 104, 118, 119, 144, 145), (124, 125, 141, 142), (),
    (129, 130), (126, 127), (), (131, 132), (), (), (133, 134, 146, 147, 148, 149), (), (), (),
    (), (), (), (), (), (), (), (), (), (), (150, 161), (), (151, 152, 162, 163), (),
    (153, 154, 164, 165, 172, 183), (), (173, 174, 184, 185), (155, 156, 166, 167),
    (186, 187, 194, 205), (), (), (175, 176), (), (), (), (), (195,),
    (157, 158, 168, 169, 196, 206, 207), (188, 189), (208, 209), (177, 178),
    (159, 170, 190, 191, 197, 198), (160,), (179, 180, 192, 210, 211), (), (171, 193, 199, 200),
    (181, 212, 213), (), (182, 201, 202, 214), (215,), (), (), (), (203,), (), (), (), (204,), (),
    (), (216, 227), (217,), (218, 228, 229, 264, 265),
    (
        219, 220, 238, 249, 230, 231, 239, 240, 250, 251, 221, 222, 232, 233, 223, 224, 234, 235,
        241, 242, 225, 236, 243, 244, 237, 245, 246, 252, 253, 247, 254, 255, 226, 256, 257, 248,
        258, 259,
    ),

)


class Place:
    def __init__(self):
        f = lax.axis_index("fsdp")
        self.z = f // (NX * NC)
        self.x = (f // NC) % NX
        self.c = f % NC
        self.y = lax.axis_index("seq")

    def at(self, z=None, x=None, c=None, y=None):
        z = self.z if z is None else z
        x = self.x if x is None else x
        c = self.c if c is None else c
        y = self.y if y is None else y
        return ((z * NX + x) * NC + c, y)

    def core(self):
        return self.at(c=1 - self.c)

    def first(self, order):
        return self.at(y=1 - self.y) if order == 0 else self.at(x=1 - self.x)

    def last(self, order):
        return self.at(x=1 - self.x) if order == 0 else self.at(y=1 - self.y)


class Gather:
    def __init__(self, me, buf, start, size, order, index, sems):
        self.me, self.buf, self.order, self.index = me, buf, order, index
        self.rows = pl.ds(start, size)
        self.sems = sems

    def own(self):
        me = self.me
        return self.buf.at[me.z, me.x, me.c, me.y, self.rows]

    def near(self):
        me = self.me
        if self.order == 0:
            return self.buf.at[me.z, me.x, me.c, 1 - me.y, self.rows]
        return self.buf.at[me.z, 1 - me.x, me.c, me.y, self.rows]

    def bundle(self, zz, far):
        me = self.me
        if self.order == 0:
            x = 1 - me.x if far else me.x
            return self.buf.at[zz, x, me.c, :, self.rows]
        y = 1 - me.y if far else me.y
        return self.buf.at[zz, :, me.c, y, self.rows]

    def quad(self, zz, other):
        c = 1 - self.me.c if other else self.me.c
        return self.buf.at[zz, :, c, :, self.rows]

    def first_copy(self, arriving=False):
        s, i = self.sems, self.index
        ref = self.near() if arriving else self.own()
        return remote(ref, ref, s.a_s.at[i], s.a_r.at[i], self.me.first(self.order))

    def line_copy(self, zz, up):
        s, i = self.sems, self.index
        ref = self.bundle(zz, False)
        step = 1 if up else -1
        return remote(
            ref,
            ref,
            (s.up_s if up else s.dn_s).at[i, zz],
            s.z_r.at[i, zz],
            self.me.at(z=self.me.z + step),
        )

    def last_copy(self, zz, arriving=False):
        s, i = self.sems, self.index
        ref = self.bundle(zz, arriving)
        return remote(ref, ref, s.b_s.at[i, zz], s.b_r.at[i, zz], self.me.last(self.order))

    def core_copy(self, zz, arriving=False):
        s, i = self.sems, self.index
        ref = self.quad(zz, arriving)
        return remote(ref, ref, s.c_s.at[i, zz], s.c_r.at[i, zz], self.me.core())

    def one_way(self, step, up, act):
        zz = self.me.z - step if up else self.me.z + step
        pl.when((zz >= 0) if up else (zz < NZ))(lambda: act(zz))

    def send_line(self, zz, up):
        z = self.me.z
        if up:

            @pl.when(z < NZ - 1)
            def _():
                self.line_copy(zz, True).start()

        else:

            @pl.when(z > 0)
            def _():
                self.line_copy(zz, False).start()

    def start(self):
        self.first_copy().start()

    def spread(self):
        self.first_copy(True).wait_recv()
        z = self.me.z
        self.send_line(z, True)
        self.send_line(z, False)
        self.last_copy(z).start()

    def line(self, step, up):
        def act(zz):
            self.line_copy(zz, up).wait_recv()
            self.send_line(zz, up)
            self.last_copy(zz).start()

        self.one_way(step, up, act)

    def cross(self, step, up):
        def act(zz):
            self.last_copy(zz, True).wait_recv()
            self.core_copy(zz).start()

        self.one_way(step, up, act)

    def finish(self):
        for zz in range(NZ):
            self.core_copy(zz, True).wait_recv()

    def events(self):
        ways = ((1, True), (1, False), (2, True), (2, False), (3, True), (3, False))
        return (
            [self.start, self.spread]
            + [functools.partial(self.line, *way) for way in ways]
            + [functools.partial(self.cross, *way) for way in ((0, True),) + ways]
        )

    def drain(self):
        z = self.me.z
        self.first_copy().wait_send()
        for zz in range(NZ):
            self.last_copy(zz).wait_send()
            self.core_copy(zz).wait_send()

            @pl.when((zz <= z) & (z < NZ - 1))
            def _():
                self.line_copy(zz, True).wait_send()

            @pl.when((zz >= z) & (z > 0))
            def _():
                self.line_copy(zz, False).wait_send()


class Scatter:
    def __init__(self, me, buf, start, size, order, index, sems, landing, out, slot, credits):
        self.me, self.buf, self.order, self.index = me, buf, order, index
        self.rows = pl.ds(start, size)
        self.sems = sems
        self.rc, self.rb, self.rz, self.ra = landing
        self.out = out
        self.slot = pl.ds(slot, size)
        self.after, self.before = credits

    def part(self, zz, far, other=False):
        me = self.me
        c = 1 - me.c if other else me.c
        if self.order == 0:
            return self.buf.at[zz, 1 - me.x if far else me.x, c, :, self.rows]
        return self.buf.at[zz, :, c, 1 - me.y if far else me.y, self.rows]

    def planes(self, far, other):
        me = self.me
        c = 1 - me.c if other else me.c
        if self.order == 0:
            return self.buf.at[:, 1 - me.x if far else me.x, c, :, self.rows]
        return self.buf.at[:, :, c, 1 - me.y if far else me.y, self.rows]

    def got_core(self, far, zz=None):
        half = 1 if far else 0
        if zz is None:
            return self.rc.at[half, :, :, self.slot]
        return self.rc.at[half, zz, :, self.slot]

    def core_copy(self, far):
        s, i = self.sems, self.index
        half = 1 if far else 0
        return remote(
            self.planes(far, True),
            self.got_core(far),
            s.rc_s.at[i, half],
            s.rc_r.at[i, half],
            self.me.core(),
        )

    def last_copy(self, zz):
        s, i = self.sems, self.index
        return remote(
            self.part(zz, True),
            self.rb.at[zz],
            s.rb_s.at[i, zz],
            s.rb_r.at[i, zz],
            self.me.last(self.order),
        )

    def line_slot(self, zz, at, down):
        return zz if down else jnp.where(zz == at, NZ, zz)

    def line_copy(self, zz, down):
        s, i = self.sems, self.index
        to = self.me.z - 1 if down else self.me.z + 1
        slot = self.line_slot(zz, to, down)
        return remote(
            self.part(zz, False),
            self.rz.at[slot],
            s.rz_s.at[i, zz],
            s.rz_r.at[i, slot],
            self.me.at(z=to),
        )

    def line_wait(self, slot):
        s, i = self.sems, self.index
        remote(
            self.rz.at[slot],
            self.rz.at[slot],
            s.rz_s.at[i, 0],
            s.rz_r.at[i, slot],
            self.me.core(),
        ).wait_recv()

    def home(self, mine):
        me = self.me
        if self.order == 0:
            y = me.y if mine else 1 - me.y
            return self.buf.at[me.z, me.x, me.c, y, self.rows], y
        x = me.x if mine else 1 - me.x
        return self.buf.at[me.z, x, me.c, me.y, self.rows], x

    def first_copy(self):
        s, i = self.sems, self.index
        return remote(
            self.home(False)[0],
            self.ra,
            s.ra_s.at[i],
            s.ra_r.at[i],
            self.me.first(self.order),
        )

    def by_distance(self, dist, act):
        act_down, act_up = (lambda zz: act(zz, True)), (lambda zz: act(zz, False))
        self.one_way(dist, True, act_down)
        if dist > 0:
            self.one_way(dist, False, act_up)

    def one_way(self, dist, down, act):
        zz = self.me.z - dist if down else self.me.z + dist
        pl.when((zz >= 0) if down else (zz < NZ))(lambda: act(zz))

    def start(self):
        if self.after is not None:
            pl.semaphore_wait(self.after, 1)
        self.core_copy(True).start()
        self.core_copy(False).start()

    def cross(self):
        self.core_copy(True).wait_recv()
        for dist in range(NZ - 1, -1, -1):

            def act(zz, down):
                ref = self.part(zz, True)
                got = self.got_core(True, zz)
                ref[...] = (ref[...].astype(F32) + got[...].astype(F32)).astype(BF16)
                self.last_copy(zz).start()

            self.by_distance(dist, act)

    def keep(self):
        self.core_copy(False).wait_recv()
        for zz in range(NZ):
            ref = self.part(zz, False)
            got = self.got_core(False, zz)
            ref[...] = (ref[...].astype(F32) + got[...].astype(F32)).astype(BF16)
        if self.before is not None:
            pl.semaphore_signal(
                self.before, inc=1, device_id=self.me.core(), device_id_type=MESH
            )

    def line(self, dist, down):
        z = self.me.z

        def act(zz):
            self.last_copy(zz).wait_recv()
            ref = self.part(zz, False)
            outer = z < NZ - 1 if down else z > 0
            total = ref[...].astype(F32) + self.rb[zz].astype(F32)

            @pl.when(outer)
            def _():
                self.line_wait(zz)
                ref[...] = (total + self.rz[zz].astype(F32)).astype(BF16)

            @pl.when(jnp.logical_not(outer))
            def _():
                ref[...] = total.astype(BF16)

            self.line_copy(zz, down).start()

        self.one_way(dist, down, act)

    def events(self):
        ways = ((3, True), (3, False), (2, True), (2, False), (1, True), (1, False))
        return (
            [self.start, self.cross, self.keep]
            + [functools.partial(self.line, *way) for way in ways]
            + [self.settle, self.finish]
        )

    def settle(self):
        z = self.me.z
        self.last_copy(z).wait_recv()
        far_ref, far = self.home(False)
        near_ref, near = self.home(True)
        self.out[self.rows, :] = near_ref[...].astype(F32) + self.rb[z, near].astype(F32)
        total = far_ref[...].astype(F32) + self.rb[z, far].astype(F32)

        @pl.when(z == 0)
        def _():
            self.line_wait(z)
            far_ref[...] = (total + self.rz[z, far].astype(F32)).astype(BF16)
            self.out[self.rows, :] += self.rz[z, near].astype(F32)

        @pl.when(z == NZ - 1)
        def _():
            self.line_wait(NZ)
            far_ref[...] = (total + self.rz[NZ, far].astype(F32)).astype(BF16)
            self.out[self.rows, :] += self.rz[NZ, near].astype(F32)

        @pl.when((z > 0) & (z < NZ - 1))
        def _():
            self.line_wait(z)
            self.line_wait(NZ)
            far_ref[...] = (
                total + (self.rz[z, far].astype(F32) + self.rz[NZ, far].astype(F32))
            ).astype(BF16)
            self.out[self.rows, :] += self.rz[z, near].astype(F32) + self.rz[NZ, near].astype(
                F32
            )

        self.first_copy().start()

    def finish(self):
        self.first_copy().wait_recv()
        self.out[self.rows, :] += self.ra[...].astype(F32)

    def drain(self):
        z = self.me.z
        self.core_copy(True).wait_send()
        self.core_copy(False).wait_send()
        self.first_copy().wait_send()
        for zz in range(NZ):
            self.last_copy(zz).wait_send()

            @pl.when(zz < z)
            def _():
                self.line_copy(zz, True).wait_send()

            @pl.when(zz > z)
            def _():
                self.line_copy(zz, False).wait_send()


class Schedule:
    def __init__(self, events):
        self.events, self.place = events, 0

    def take(self):
        chosen = PLAN[self.place]
        self.place += 1

        def run():
            for number in chosen:
                self.events[number]()

        return run if chosen else None

    def step(self, count=1):
        for _ in range(count):
            run = self.take()
            if run is not None:
                run()

    def loop(self, count, body):
        runs = [self.take() for _ in range(count)]

        @pl.loop(0, count)
        def _(i):
            body(i)
            for place, run in enumerate(runs):
                if run is not None:
                    pl.when(i == place)(run)


def repeat(count, body):
    pl.loop(0, count)(body)


def flatten(value):
    return value.reshape(-1, value.shape[-1])


def attention_pair(queries, keys, values, bias):
    first = lax.broadcasted_iota(jnp.int32, keys.shape, 1) < HEAD_DIM
    zero = jnp.zeros((), BF16)
    values_turned = values.T
    contexts, totals = [], []
    for half in range(2):
        keys_half = jnp.where(first if half == 0 else ~first, keys, zero)
        scores = nt_dot(keys_half, queries) + bias
        largest = jnp.max(scores, axis=0, keepdims=True)
        exponent = jnp.exp(scores - largest)
        total = column_sum(exponent)
        soft = (exponent * (1.0 / total)).astype(BF16)
        contexts.append(
            plain_dot(values_turned[half * HEAD_DIM : (half + 1) * HEAD_DIM, :], soft)
        )
        totals.append(largest + jnp.log(total))
    return jnp.concatenate(contexts, 0).T, jnp.concatenate(totals, 0)


def attention_pair_back(queries, keys, values, grad_context, bias, log_total):
    first = lax.broadcasted_iota(jnp.int32, keys.shape, 1) < HEAD_DIM
    zero = jnp.zeros((), BF16)
    keys_turned = keys.T
    grad_queries = []
    grad_keys = grad_values = 0.0
    for half in range(2):
        mask = first if half == 0 else ~first
        scores = nt_dot(jnp.where(mask, keys, zero), queries) + bias
        soft = jnp.exp(scores - log_total[half : half + 1, :])
        grad_soft = nt_dot(jnp.where(mask, values, zero), grad_context)
        inner = column_sum(soft * grad_soft)
        grad_scores = (soft * (grad_soft - inner)).astype(BF16)
        grad_values += plain_dot(soft.astype(BF16), jnp.where(mask, grad_context, zero))
        grad_keys += plain_dot(grad_scores, jnp.where(mask, queries, zero))
        grad_queries.append(
            plain_dot(keys_turned[half * HEAD_DIM : (half + 1) * HEAD_DIM, :], grad_scores)
        )
    return jnp.concatenate(grad_queries, 0).T, grad_keys, grad_values


def select_columns(permuted):
    row = lax.broadcasted_iota(jnp.int32, (8 * 128, D), 0)
    col = lax.broadcasted_iota(jnp.int32, (8 * 128, D), 1)
    lane = row % 128
    source = (row // 128) * SHARD_A + lane
    if permuted:
        piece = col // 256
        rest = col % 256
        col = (rest // PIECE) * SHARD_F + piece * PIECE + rest % PIECE
    return jnp.where((source == col) & (lane < SHARD_A), 1.0, 0.0).astype(BF16)


SEM_SHAPES = dict(
    a_s=(10,),
    a_r=(10,),
    z_r=(10, NZ),
    up_s=(10, NZ),
    dn_s=(10, NZ),
    b_s=(10, NZ),
    b_r=(10, NZ),
    c_s=(10, NZ),
    c_r=(10, NZ),
    rc_s=(10, 2),
    rc_r=(10, 2),
    rb_s=(10, NZ),
    rb_r=(10, NZ),
    rz_s=(10, NZ),
    rz_r=(10, NZ + 1),
    ra_s=(10,),
    ra_r=(10,),
    x_s=(4, 2),
    x_r=(4, 2),
    own=(4, 2),
    pool_s=(1,),
    pool_r=(1,),
    stat_s=(5,),
    stat_r=(5,),
    load=(3,),
)


def pieces():
    rest = PIECE - SPLIT_F
    return [(0, SPLIT_F, rest), (PIECE, FULL_A - PIECE - rest, rest)] + [
        (k * PIECE, SPLIT_F, rest) for k in range(PIECES)
    ]


def scratch():
    return dict(
        wa=pltpu.VMEM((NZ, NX, NC, NY, FULL_A, D), BF16),
        wf=pltpu.VMEM((NZ, NX, NC, NY, SHARD_F, D), BF16),
        rc=pltpu.VMEM((2, NZ, 2, PIECE, D), BF16),
        xs=pltpu.VMEM((TOKENS, D), BF16),
        dys=pltpu.VMEM((TOKENS, D), BF16),
        ctx=pltpu.VMEM((TOKENS, D), BF16),
        n1=pltpu.VMEM((TOKENS, D), BF16),
        fn=pltpu.VMEM((TOKENS, D), BF16),
        fg=pltpu.VMEM((TOKENS, D), BF16),
        qkv=pltpu.VMEM((TOKENS, 3 * D), BF16),
        act=pltpu.VMEM((PIECES, TOKENS, BLOCK), BF16),
        slope=pltpu.VMEM((PIECES, TOKENS, BLOCK), BF16),
        acc=pltpu.VMEM((TOKENS, D), F32),
        bias=pltpu.VMEM((OWN_ROWS, ROW, ROW), BF16),
        totals=pltpu.VMEM((OWN_ROWS * HEADS // 2, 2, ROW), F32),
        side=pltpu.VMEM((TOKENS, 128), F32),
        vec=pltpu.VMEM((16, 4 * D), F32),
        bu=pltpu.VMEM((PIECES, 16, BLOCK), F32),
        gvec=pltpu.VMEM((8, 4 * D), F32),
        gbu=pltpu.VMEM((PIECES, 8, BLOCK), F32),
        stat=pltpu.VMEM((8, 128), F32),
        stat_in=pltpu.VMEM((5, 8, 128), F32),
        pool_out=pltpu.VMEM((OWN_ROWS, 8, D), F32),
        pool_in=pltpu.VMEM((OWN_ROWS, 8, D // 2), F32),
        credit=pltpu.SemaphoreType.REGULAR((2,)),
        free=pltpu.SemaphoreType.REGULAR,
    )


def landing_shapes():
    shapes = []
    for _ in range(PIECES):
        for size in (SPLIT_F, PIECE - SPLIT_F):
            shapes += [
                pltpu.VMEM((NZ, 2, size, D), BF16),
                pltpu.VMEM((NZ + 1, 2, size, D), BF16),
                pltpu.VMEM((size, D), BF16),
            ]
    return shapes


def fused_kernel(
    x_in,
    dy_in,
    wa_in,
    wf_in,
    ids,
    flags,
    flag_column,
    out_y,
    out_dx,
    out_pooled,
    out_stats,
    grad_a,
    grad_f,
    *more,
):
    names, sem_names = tuple(scratch()), tuple(SEM_SHAPES)
    landings = len(landing_shapes())
    r = types.SimpleNamespace(**dict(zip(names, more)))
    landing_refs = more[len(names) : len(names) + landings]
    sems = types.SimpleNamespace(**dict(zip(sem_names, more[len(names) + landings :])))
    me = Place()
    z, x, c, y = me.z, me.x, me.c, me.y
    wa, wf, xs, dys, ctx = r.wa, r.wf, r.xs, r.dys, r.ctx
    n1, fn, fg, qkv, acc = r.n1, r.fn, r.fg, r.qkv, r.acc
    act, slope, vec, gvec, stat = r.act, r.slope, r.vec, r.gvec, r.stat

    def tile(i, size):
        return pl.ds(pl.multiple_of(i * size, size), size)

    def vector(row, quarter):
        return vec[row : row + 1, quarter * D : (quarter + 1) * D]

    barrier = pltpu.get_barrier_semaphore()
    for where in (
        me.core(),
        me.at(x=1 - x),
        me.at(y=1 - y),
        me.at(z=(z + 2) % NZ),
    ):
        pl.semaphore_signal(barrier, inc=1, device_id=where, device_id_type=MESH)

    @pl.when(z > 0)
    def _():
        pl.semaphore_signal(barrier, inc=1, device_id=me.at(z=z - 1), device_id_type=MESH)

    @pl.when(z < NZ - 1)
    def _():
        pl.semaphore_signal(barrier, inc=1, device_id=me.at(z=z + 1), device_id_type=MESH)

    load_a = pltpu.make_async_copy(wa_in, wa.at[z, x, c, y], sems.load.at[0])
    load_f = pltpu.make_async_copy(wf_in, wf.at[z, x, c, y], sems.load.at[1])
    load_s = pltpu.make_async_copy(flag_column, r.side, sems.load.at[2])
    load_a.start()
    load_f.start()
    load_s.start()

    def row_copy(kind, src, dst, slot):
        return remote(
            src, dst, sems.x_s.at[kind, slot], sems.x_r.at[kind, slot], me.at(y=1 - y)
        )

    def own_copy(kind, src, dst, slot):
        return pltpu.make_async_copy(src, dst, sems.own.at[kind, slot])

    def span(slot, half):
        return pl.ds(pl.multiple_of(slot * ROW + half * (ROW // 2), ROW // 2), ROW // 2)

    def take_rows(kind, source, target):
        sends = [
            row_copy(kind, source.at[2 * (1 - y) + slot], target.at[span(slot, y)], slot)
            for slot in range(OWN_ROWS)
        ]
        owns = [
            own_copy(kind, source.at[2 * y + slot], target.at[span(slot, y)], slot)
            for slot in range(OWN_ROWS)
        ]
        arrivals = [
            row_copy(kind, source.at[2 * y + slot], target.at[span(slot, 1 - y)], slot)
            for slot in range(OWN_ROWS)
        ]
        return sends, owns, arrivals

    def give_rows(kind, source, target):
        sends = [
            row_copy(kind, source.at[span(slot, 1 - y)], target.at[2 * y + slot], slot)
            for slot in range(OWN_ROWS)
        ]
        owns = [
            own_copy(kind, source.at[span(slot, y)], target.at[2 * y + slot], slot)
            for slot in range(OWN_ROWS)
        ]
        arrivals = [
            row_copy(kind, source.at[span(slot, y)], target.at[2 * (1 - y) + slot], slot)
            for slot in range(OWN_ROWS)
        ]
        return sends, owns, arrivals

    x_sends, x_owns, x_arrivals = take_rows(0, x_in, xs)
    dy_sends, dy_owns, dy_arrivals = take_rows(1, dy_in, dys)
    out_sends, out_owns, out_arrivals = give_rows(2, dys, out_y)
    dx_sends, dx_owns, dx_arrivals = give_rows(3, n1, out_dx)

    def start_all(copies):
        def run():
            for copy in copies:
                copy.start()

        return run

    gathers, scatters = [], []
    for piece, (first_row, *sizes) in enumerate(pieces()):
        for order in range(2):
            buf = wa if piece < 2 else wf
            start = first_row + order * sizes[0]
            gathers.append(Gather(me, buf, start, sizes[order], order, 2 * piece + order, sems))
    for piece, (first_row, *sizes) in enumerate(pieces()[2:] + pieces()[:2]):
        out = grad_f if piece < PIECES else grad_a
        for order in range(2):
            size, i = sizes[order], 2 * (piece % PIECES) + order
            landing = (
                r.rc,
                landing_refs[3 * i].at[:, :, 0:size],
                landing_refs[3 * i + 1].at[:, :, 0:size],
                landing_refs[3 * i + 2].at[0:size],
            )
            credit = r.credit.at[order]
            credits = (credit if piece > 0 else None, credit if piece < PIECES + 1 else None)
            slot = order * sizes[0]
            scatters.append(
                Scatter(
                    me, wf, first_row + slot, size, order, 2 * piece + order, sems, landing, out,
                    slot, credits,
                )
            )

    exchange = [copy.start for copy in x_sends + dy_sends + dx_sends]
    events = [event for one in gathers + scatters for event in one.events()] + exchange
    plan = Schedule(events)

    for copy in x_owns + dy_owns:
        copy.start()
    line_ends = jnp.where(z > 0, 1, 0).astype(jnp.int32) + jnp.where(z < NZ - 1, 1, 0).astype(
        jnp.int32
    )
    load_a.wait()
    pl.semaphore_wait(barrier, 4 + line_ends)
    plan.step()
    load_f.wait()

    gvec[...] = jnp.zeros_like(gvec)
    r.gbu[...] = jnp.zeros_like(r.gbu)
    stat[...] = jnp.zeros_like(stat)
    for slot in range(OWN_ROWS):
        wide = jnp.broadcast_to(ids[slot].astype(F32), (128, ROW))
        tall = wide.T
        for j in range(ROW // 128):
            across = wide[:, j * 128 : (j + 1) * 128]
            across = jnp.broadcast_to(across[0:1, :], (ROW, 128))
            r.bias[slot, :, j * 128 : (j + 1) * 128] = jnp.where(
                tall == across, 0.0, masked_score
            ).astype(BF16)
        plan.step()
    ctx[...] = select_columns(False)
    fg[...] = select_columns(True)
    plan.step()
    plan.step()
    for one in gathers[:4]:
        one.finish()

    for q in range(4):
        blocks = jnp.concatenate(
            [
                wa[q, j // 4, (j // 2) % 2, j % 2, SHARD_A:FULL_A, 0:128]
                for j in range(8)
            ],
            axis=1,
        )
        vec[:, q * D : (q + 1) * D] = plain_dot(blocks, ctx[...])
        moved = plain_dot(blocks, fg[...])
        for k in range(PIECES):
            r.bu[k, :, q * 256 : (q + 1) * 256] = moved[:, k * 256 : (k + 1) * 256]

    plan.step()
    load_s.wait()
    plan.step()
    for copy in x_owns:
        copy.wait()
    for copy in x_arrivals:
        copy.wait_recv()

    scale = HEAD_DIM ** (-0.5)

    def project(i):
        rows = tile(i, 512)
        tokens = xs[rows, :]
        wide = tokens.astype(F32)
        stat[0:1, :] += lane_sums(wide * wide * r.side[rows, 1:2])
        for j in range(3):
            weights = flatten(wa[j, :, :, :, 0:SHARD_A, :])
            value = nt_dot(tokens, weights)
            if j == 0:
                value = (value + vector(0, 0)) * scale
            if j == 2:
                value = value + vector(0, 1)
            qkv[rows, j * D : (j + 1) * D] = value.astype(BF16)

    def lane_sums(value):
        total = column_sum(value)
        return sum(total[:, j * 128 : (j + 1) * 128] for j in range(D // 128))

    plan.loop(2, project)

    def columns(pair, block):
        return pl.ds(pl.multiple_of(block * D + pair * 128, 128), 128)

    def attend(i):
        slot, pair = i // (HEADS // 2), i % (HEADS // 2)
        rows = tile(slot, ROW)
        context, total = attention_pair(
            qkv[rows, columns(pair, 0)],
            qkv[rows, columns(pair, 1)],
            qkv[rows, columns(pair, 2)],
            r.bias[slot].astype(F32),
        )
        ctx[rows, columns(pair, 0)] = context.astype(BF16)
        r.totals[i] = total

    plan.loop(OWN_ROWS * HEADS // 2, attend)

    def attention_output(i):
        rows = tile(i, 256)
        weights = flatten(wa[3, :, :, :, 0:SHARD_A, :])
        out = nt_dot(ctx[rows, :], weights) + vector(0, 2)
        stat[1:2, :] += lane_sums(out * out * r.side[rows, 1:2])
        normed, inverse = normalize(xs[rows, :].astype(F32) + out)
        n1[rows, :] = normed.astype(BF16)
        r.side[rows, 0:1] = inverse
        fn[rows, :] = (normed * vector(2, 0) + vector(2, 1)).astype(BF16)

    plan.loop(4, attention_output)

    def up_rows(k):
        return flatten(flatten_lead(wf[0:2, :, :, :, k * PIECE : (k + 1) * PIECE, :]))

    def down_rows(k):
        return flatten(flatten_lead(wf[2:4, :, :, :, k * PIECE : (k + 1) * PIECE, :]))

    def flatten_lead(value):
        return value.reshape(-1, PIECE, D)

    for k in range(PIECES):
        plan.step()
        for one in gathers[4 + 2 * k : 6 + 2 * k]:
            one.finish()

        def feed(i, k=k):
            rows = tile(i, 512)
            up = nt_dot(fn[rows, :], up_rows(k)) + r.bu[k, 1:2, :]
            half = 0.5 * (1.0 + lax.erf(up * math.sqrt(0.5)))
            activated = (up * half).astype(BF16)
            act[k, rows, :] = activated
            slope[k, rows, :] = (
                half + up * (jnp.exp(-0.5 * up * up) * (1.0 / math.sqrt(2.0 * math.pi)))
            ).astype(BF16)
            value = plain_dot(activated, down_rows(k))
            if k == 0:
                acc[rows, :] = value
            else:
                acc[rows, :] += value

        plan.loop(2, feed)
    plan.step()

    for copy in dy_owns:
        copy.wait()
    for copy in dy_arrivals:
        copy.wait_recv()
    for one in gathers:
        one.drain()

    def second(i):
        rows = tile(i, 128)
        feed_out = acc[rows, :] + vector(0, 3)
        stat[2:3, :] += lane_sums(feed_out * feed_out * r.side[rows, 1:2])
        normed, inverse = normalize(fn[rows, :].astype(F32) + feed_out)
        grad = dys[rows, :].astype(F32)
        dys[rows, :] = (normed * vector(2, 2) + vector(2, 3)).astype(BF16)
        gvec[2:3, 2 * D : 3 * D] += column_sum(grad * normed)
        gvec[2:3, 3 * D :] += column_sum(grad)
        back = norm_back(grad * vector(2, 2), normed, inverse)
        acc[rows, :] = back
        low = back.astype(BF16)
        fg[rows, :] = low
        gvec[0:1, 3 * D :] += column_sum(low.astype(F32))

    repeat(TOKENS // 128, second)
    plan.step()

    start_all(out_sends + out_owns)()

    segments = lax.broadcasted_iota(jnp.int32, (SEGMENTS, ROW), 0)
    for slot in range(OWN_ROWS):
        member = jnp.where(segments == ids[slot], 1.0, 0.0) * flags[slot]
        sums = plain_dot(member.astype(BF16), dys[slot * ROW : (slot + 1) * ROW, :])
        counts = jnp.sum(member, axis=1, keepdims=True)
        r.pool_out[slot] = sums / jnp.maximum(counts, 1.0)
        total = flags[slot]
        stat[3:4, :] += sum(total[:, j * 128 : (j + 1) * 128] for j in range(ROW // 128))

    def half_lanes(which):
        return pl.ds(pl.multiple_of(which * (D // 2), 128), D // 2)

    pool_copy = remote(
        r.pool_out.at[:, :, half_lanes(1 - y)],
        r.pool_in,
        sems.pool_s.at[0],
        sems.pool_r.at[0],
        me.at(y=1 - y),
    )
    pool_copy.start()

    stat_partners = [
        me.core(),
        me.at(x=1 - x),
        me.at(y=1 - y),
        me.at(z=z + 1 - 2 * (z % 2)),
        me.at(z=(z + 2) % NZ),
    ]

    def stat_copy(step):
        return remote(
            stat,
            r.stat_in.at[step],
            sems.stat_s.at[step],
            sems.stat_r.at[step],
            stat_partners[step],
        )

    def stat_start(step):
        return lambda: stat_copy(step).start()

    def stat_end(step):
        def run():
            stat_copy(step).wait()
            stat[...] += r.stat_in[step]

        return run

    stat_start(0)()
    plan.step()
    for k in range(PIECES):

        def feed_back(i, k=k):
            rows = tile(i, 512)
            grad = nt_dot(fg[rows, :], down_rows(k)) * slope[k, rows, :].astype(F32)
            low = grad.astype(BF16)
            slope[k, rows, :] = low
            r.gbu[k, 0:1, :] += column_sum(low.astype(F32))
            acc[rows, :] += plain_dot(low, up_rows(k))

        plan.loop(2, feed_back)

        def weights_back(i, k=k):
            cols = tile(i, BLOCK // 2)
            down = tn_dot(act[k, :, cols], fg[...]).astype(BF16)
            up = tn_dot(slope[k, :, cols], fn[...]).astype(BF16)
            where = (slice(None), slice(None), slice(None), pl.ds(k * PIECE, PIECE))
            wf[(2 + i, *where)] = down.reshape(NX, NC, NY, PIECE, D)
            wf[(i, *where)] = up.reshape(NX, NC, NY, PIECE, D)

        plan.loop(2, weights_back)
        stat_end(k)()
        stat_start(k + 1)()

    def first(i):
        rows = tile(i, 128)
        grad = acc[rows, :]
        normed = n1[rows, :].astype(F32)
        gvec[2:3, 0:D] += column_sum(grad * normed)
        gvec[2:3, D : 2 * D] += column_sum(grad)
        stream = norm_back(grad * vector(2, 0), normed, r.side[rows, 0:1])
        acc[rows, :] = stream
        low = stream.astype(BF16)
        fg[rows, :] = low
        gvec[0:1, 2 * D : 3 * D] += column_sum(low.astype(F32))

    plan.loop(TOKENS // 128, first)

    def context_back(i):
        rows = tile(i, 512)
        fn[rows, :] = plain_dot(fg[rows, :], flatten(wa[3, :, :, :, 0:SHARD_A, :])).astype(BF16)

    plan.loop(2, context_back)
    stat_end(3)()
    stat_start(4)()

    def attend_back_pair(i):
        slot, pair = i // (HEADS // 2), i % (HEADS // 2)
        rows = tile(slot, ROW)
        grads = attention_pair_back(
            qkv[rows, columns(pair, 0)],
            qkv[rows, columns(pair, 1)],
            qkv[rows, columns(pair, 2)],
            fn[rows, columns(pair, 0)],
            r.bias[slot].astype(F32),
            r.totals[i],
        )
        for j in range(3):
            low = grads[j].astype(BF16)
            if j == 0:
                low = low * jnp.asarray(scale, BF16)
            qkv[rows, columns(pair, j)] = low
            if j != 1:
                gvec[0:1, columns(pair, j // 2)] += column_sum(low.astype(F32))

    plan.loop(OWN_ROWS * HEADS // 2, attend_back_pair)
    stat_end(4)()
    plan.step()
    for one in scatters[:4]:
        one.drain()

    free = r.free
    for where in (me.at(x=1 - x), me.at(y=1 - y)):
        pl.semaphore_signal(free, inc=1, device_id=where, device_id_type=MESH)

    @pl.when(z > 0)
    def _():
        pl.semaphore_signal(free, inc=1, device_id=me.at(z=z - 1), device_id_type=MESH)

    @pl.when(z < NZ - 1)
    def _():
        pl.semaphore_signal(free, inc=1, device_id=me.at(z=z + 1), device_id_type=MESH)

    for j in range(3):

        def inner_back(i, j=j):
            cols = pl.ds(pl.multiple_of(j * D + i * (D // 2), 128), D // 2)
            value = tn_dot(qkv[:, cols], xs[...]).astype(BF16)
            wf[j, i, :, :, 0:SHARD_A, :] = value.reshape(NC, NY, SHARD_A, D)

        plan.loop(2, inner_back)

    def outer_back(i):
        cols = pl.ds(pl.multiple_of(i * (D // 2), 128), D // 2)
        value = tn_dot(fg[:, cols], ctx[...]).astype(BF16)
        wf[3, i, :, :, 0:SHARD_A, :] = value.reshape(NC, NY, SHARD_A, D)

    plan.loop(2, outer_back)
    pl.semaphore_wait(free, 2 + line_ends)

    ctx[...] = select_columns(False)
    fg[...] = select_columns(True)
    row = lax.broadcasted_iota(jnp.int32, (8, 1), 0)
    for q in range(4):
        plain = nt_dot(gvec[:, q * D : (q + 1) * D].astype(BF16), ctx[...])
        piled = jnp.concatenate(
            [r.gbu[k, :, q * 256 : (q + 1) * 256] for k in range(PIECES)], axis=1
        )
        moved = nt_dot(piled.astype(BF16), fg[...])
        low = jnp.where(row == 1, jnp.broadcast_to(moved[0:1, :], plain.shape), plain)
        low = jnp.concatenate([low, jnp.zeros_like(low)], axis=0).astype(BF16)
        for j in range(8):
            wf[q, j // 4, (j // 2) % 2, j % 2, SHARD_A:FULL_A, 0:128] = low[
                :, j * 128 : (j + 1) * 128
            ]
    plan.step()

    def input_back(i):
        rows = tile(i, 512)
        value = acc[rows, :]
        for j in range(3):
            value += plain_dot(
                qkv[rows, j * D : (j + 1) * D], flatten(wa[j, :, :, :, 0:SHARD_A, :])
            )
        n1[rows, :] = value.astype(BF16)

    plan.loop(2, input_back)
    start_all(dx_owns)()
    plan.step()

    for one in scatters[4:]:
        one.drain()
    pool_copy.wait()
    for slot in range(OWN_ROWS):
        out_pooled[2 * y + slot] = r.pool_out[slot, :, half_lanes(y)]
        out_pooled[2 * (1 - y) + slot] = r.pool_in[slot]
    out_stats[...] = stat[...]
    for copies in (x_sends, dy_sends, out_sends, dx_sends):
        for copy in copies:
            copy.wait_send()
    for copies in (out_owns, dx_owns):
        for copy in copies:
            copy.wait()
    for copies in (out_arrivals, dx_arrivals):
        for copy in copies:
            copy.wait_recv()


def fused_call(inputs, output_grad, attention_low, feedforward_low, ids, flags, flag_column):
    row_count, local_span, width = inputs.shape
    any_space = pl.BlockSpec(memory_space=pl.ANY)
    vmem = pl.BlockSpec(memory_space=pltpu.VMEM)
    semaphores = [pltpu.SemaphoreType.DMA(shape) for shape in SEM_SHAPES.values()]
    return pl.pallas_call(
        fused_kernel,
        out_shape=(
            jax.ShapeDtypeStruct(inputs.shape, BF16),
            jax.ShapeDtypeStruct(inputs.shape, BF16),
            jax.ShapeDtypeStruct((row_count, SEGMENTS, D // NY), F32),
            jax.ShapeDtypeStruct((8, 128), F32),
            jax.ShapeDtypeStruct((FULL_A, D), F32),
            jax.ShapeDtypeStruct((SHARD_F, D), F32),
        ),
        in_specs=[any_space] * 4 + [vmem] * 2 + [any_space],
        out_specs=(any_space, any_space, vmem, vmem, vmem, vmem),
        scratch_shapes=list(scratch().values()) + landing_shapes() + semaphores,
        compiler_params=pltpu.CompilerParams(
            collective_id=0, has_side_effects=True, vmem_limit_bytes=65_000 * 1024
        ),
        name="layer",
    )(inputs, output_grad, attention_low, feedforward_low, ids, flags, flag_column)


def fused_shards(
    inputs,
    segment_ids,
    token_flags,
    output_grad,
    attention_weights,
    feedforward_weights,
    layer_vectors,
    attention_first,
    attention_second,
    feedforward_first,
    feedforward_second,
    vector_first,
    vector_second,
):
    seq = lax.axis_index("seq")
    ids = lax.dynamic_slice_in_dim(segment_ids, seq * OWN_ROWS, OWN_ROWS, 0)
    flags = lax.dynamic_slice_in_dim(token_flags, seq * OWN_ROWS, OWN_ROWS, 0).astype(F32)
    flag_column = jnp.broadcast_to(flags.reshape(TOKENS, 1), (TOKENS, 128))
    vector_rows = jnp.pad(layer_vectors, ((0, EXTRA - 3), (0, D - SHARD_A)))
    attention_low = jnp.concatenate([attention_weights.T, vector_rows], axis=0).astype(BF16)
    feedforward_low = feedforward_weights.T.astype(BF16)
    output_rows, input_rows, pooled, stats, grad_a, grad_f = fused_call(
        inputs,
        output_grad,
        attention_low,
        feedforward_low,
        ids.reshape(OWN_ROWS, 1, ROW),
        flags.reshape(OWN_ROWS, 1, ROW),
        flag_column,
    )
    totals = jnp.sum(stats[0:4], axis=1)
    stream_rms = jnp.sqrt(totals[0:3] / D / totals[3])
    attention_new = adamw_update(
        attention_weights,
        grad_a[0:SHARD_A].T,
        attention_first,
        attention_second,
        rate_attention,
        weight_decay,
    )
    feedforward_new = adamw_update(
        feedforward_weights,
        grad_f.T,
        feedforward_first,
        feedforward_second,
        rate_feedforward,
        weight_decay,
    )
    vectors_new = adamw_update(
        layer_vectors,
        grad_a[SHARD_A : SHARD_A + 3, 0:SHARD_A],
        vector_first,
        vector_second,
        rate_vectors,
        0.0,
    )
    return (
        output_rows,
        input_rows,
        pooled,
        stream_rms,
        *attention_new,
        *feedforward_new,
        *vectors_new,
    )


def solution(mesh):
    fused = mesh.shape["fsdp"] == NZ * NX * NC and mesh.shape["seq"] == NY
    rows = P("fsdp", "seq", None)
    table = P("fsdp", None)
    owned = P(None, ("fsdp", "seq"))
    return jax.shard_map(
        fused_shards if fused else plain_shards,
        mesh=mesh,
        in_specs=(rows, table, table, rows) + (owned,) * 9,
        out_specs=(rows, rows, P("fsdp", None, "seq"), P()) + (owned,) * 12,
        check_vma=False,
    )
```

profile of v0, /device:TPU:0, one launch (start us, length us, event | category | flops | bytes accessed | tf_op | source)
XLA Modules:
  0.0 233.9 jit_solution(7611254569582817933)
XLA Ops:
  0.6 0.7 convert.10
  1.3 0.7 dynamic-slice_convert_fusion
  2.1 0.6 reshape.40.ids
  2.7 0.6 reshape.41.flags
  3.3 1.0 convert_bitcast_fusion.1
  4.2 0.7 fusion.3.wa_in
  4.9 1.8 convert_bitcast_fusion.wf_in
  6.7 1.0 broadcast_in_dim.8.flag_column
  7.7 0.0 copy-start.7
  7.7 0.0 copy-start.8
  7.7 0.0 copy-start.9
  7.7 0.0 copy-start.3
  7.7 213.2 %layer.1 = (bf16[4,256,768]{2,1,0:T(8,128)(2,1)}, bf16[4,256,768]{2,1,0:T(8,128)(2,1)}, f32[4,8,384]{2,1,0:T(8,128)}, f32[8,128]{1,0:T(8,128)}, f32[112,768]{1,0:T(8,128)}, /*index=5*/f32[192,768]{1,0:T(8,128)}) custom-call(bf16[4,256,768]{2,1,0:T(8,128)(2,1)} %x_in.1, bf16[4,256,768]{2,1,0:T(8,128)(2,1)} %dy_in.1, bf16[112,768]{1,0:T(8,128)(2,1)} %fusion.3.wa_in, ...), custom_call_target="tpu_custom_call" | custom-call | tf_op jit(solution)/shard_map/layer/pallas_call | solution.py:1456
  220.9 0.0 copy-start
  220.9 0.0 copy-start.4
  220.9 0.0 copy-start.5
  221.0 0.9 slice_reduce_fusion
  221.9 0.6 slice.17
  222.5 1.2 divide_sqrt_fusion
  223.6 0.0 copy-done.7
  223.6 0.0 copy-done.8
  223.6 0.0 copy-done.9
  223.6 1.3 fusion.5
  224.9 0.0 copy-done.3
  224.9 2.2 fusion.9
  227.2 0.0 copy-done
  227.2 0.0 copy-done.4
  227.2 0.0 copy-done.5
  227.2 0.0 copy-start.2
  227.2 2.8 %fusion.7 = (bf16[768,192]{0,1:T(8,128)(2,1)}, f32[768,192]{0,1:T(8,128)}, f32[768,192]{0,1:T(8,128)}, f32[768,192]{0,1:T(8,128)}) fusion(f32[768,192]{0,1:T(8,128)S(1)} %copy-done, f32[192,768]{1,0:T(8,128)} %get-tuple-element.27, f32[768,192]{0,1:T(8,128)S(1)} %copy-done.4, f32[768,192]{0,1:T(8,128)S(1)} %copy-done.5), kind=kLoop, calls=%fused_computation.22 | loop fusion | flops 2211840 | bytes 4423680 | tf_op jit(solution)/shard_map/convert_element_type | solution.py:121
  230.0 0.0 copy-done.2
  230.0 0.0 copy-start.1
  230.0 1.1 copy.33
  231.2 0.8 copy-done.1
  232.0 0.0 copy-start.6
  232.0 1.1 copy.34
  233.1 0.0 copy-done.6
  233.1 0.6 copy.35
  (1 shorter events, 0.0 us)
Async XLA Ops:
  7.7 215.9 %copy-start.7 = (f32[3,96]{1,0:T(4,128)S(1)}, f32[3,96]{1,0:T(4,128)}, u32[]{:S(2)}) copy-start(f32[3,96]{1,0:T(4,128)} %param.19) | copy-start | bytes 3460
  7.7 215.9 %copy-start.8 = (f32[3,96]{1,0:T(4,128)S(1)}, f32[3,96]{1,0:T(4,128)}, u32[]{:S(2)}) copy-start(f32[3,96]{1,0:T(4,128)} %param.24) | copy-start | bytes 3460
  7.7 215.9 %copy-start.9 = (f32[3,96]{1,0:T(4,128)S(1)}, f32[3,96]{1,0:T(4,128)}, u32[]{:S(2)}) copy-start(f32[3,96]{1,0:T(4,128)} %param.25) | copy-start | bytes 3460
  7.7 217.2 %copy-start.3 = (f32[768,96]{0,1:T(8,128)S(1)}, f32[768,96]{0,1:T(8,128)}, u32[]{:S(2)}) copy-start(f32[768,96]{0,1:T(8,128)} %param.17) | copy-start | bytes 884740
  220.9 6.3 %copy-start = (f32[768,192]{0,1:T(8,128)S(1)}, f32[768,192]{0,1:T(8,128)}, u32[]{:S(2)}) copy-start(f32[768,192]{0,1:T(8,128)} %param.18) | copy-start | bytes 1769476
  220.9 6.2 %copy-start.4 = (f32[768,192]{0,1:T(8,128)S(1)}, f32[768,192]{0,1:T(8,128)}, u32[]{:S(2)}) copy-start(f32[768,192]{0,1:T(8,128)} %param.22) | copy-start | bytes 1769476
  220.9 6.2 %copy-start.5 = (f32[768,192]{0,1:T(8,128)S(1)}, f32[768,192]{0,1:T(8,128)}, u32[]{:S(2)}) copy-start(f32[768,192]{0,1:T(8,128)} %param.23) | copy-start | bytes 1769476
  227.2 2.8 %copy-start.2 = (bf16[4,256,768]{2,1,0:T(8,128)(2,1)S(1)}, bf16[4,256,768]{2,1,0:T(8,128)(2,1)}, u32[]{:S(2)}) copy-start(bf16[4,256,768]{2,1,0:T(8,128)(2,1)} %get-tuple-element.58) | copy-start | bytes 4718596
  230.0 2.0 copy-start.1
  232.0 1.1 copy-start.6
where the time goes:
time: 238 us; the launch traced here: 234 us
  Pallas kernels  213 us (89%)
  other arithmetic  13.3 us (6%)
  local copies, waits for them, and re-layouts  6.55 us (3%)
    pallas_call x1, Pallas kernels, fused_call(): pl.pallas_call(fused_kernel, out_shape=(jax.ShapeDtypeStruct(inputs.shape...  213 us
    convert_element_type x3, other arithmetic, adamw_update(): return (weight_new, first_new, second_new, weight_new.astype(jnp.bfloat16))  6.35 us

commit v1 on v0

--- a/solution.py
+++ b/solution.py
@@ -352,6 +352,10 @@
 PIECE = SHARD_F // PIECES
 BLOCK = FF // PIECES
 SPLIT_F = 48
+SIZES_F = (SPLIT_F, PIECE - SPLIT_F)
+GATHER_A = ((48, 16), (32, 16))
+SCATTER_A = ((48, 16), (32, 16))
+SCATTER_O = (64, 48)
 
 
 def tn_dot(left_side, right_side):
@@ -382,30 +386,29 @@
 
 
 PLAN = (
-    (0, 15, 30, 45), (), (16, 260), (1,),
+    (0, 15, 30, 45), (), (16, 282), (1,), (),
     (
-        17, 18, 23, 46, 60, 75, 2, 3, 8, 31, 19, 20, 261, 47, 48, 9, 4, 5,
-        24, 32, 33, 25, 90, 105, 10, 21, 22, 53, 49, 50, 76, 38, 26, 27, 6, 7,
-        34, 35, 61, 11, 12, 51, 52, 77, 78, 39, 40, 13, 14, 36, 37, 41, 42, 54,
-        55, 62, 63, 28, 29, 120, 135, 68, 79, 80, 106, 56, 57, 43, 44, 83, 58, 59,
-        64, 65, 91,
+        17, 18, 23, 46, 2, 3, 8, 31, 60, 75, 19, 20, 47, 48, 9, 4, 5, 32,
+        33, 90, 105, 10, 21, 22, 283, 49, 50, 38, 6, 7, 28, 29, 34, 35, 24, 51,
+        52, 11, 12, 76, 25, 53, 13, 14, 36, 37, 39, 40, 61, 77, 78, 106, 26, 27,
+        41, 42, 43, 44, 54, 55, 62, 63, 91, 120, 135, 79, 80, 58, 59, 56, 57, 68,
+        83, 107, 108,
     ),
-    (81, 82, 84, 85, 86, 87, 107, 108), (), (66, 67, 69, 70, 88, 89, 113),
-    (71, 72, 92, 93, 114, 115), (98, 109, 110, 136), (73, 74, 262),
-    (94, 95, 111, 112, 99, 117, 116, 121, 138, 137, 143), (100,), (96, 97, 263), (101, 102),
-    (122, 123), (128, 139, 140), (103, 104, 118, 119, 144, 145), (124, 125, 141, 142), (),
-    (129, 130), (126, 127), (), (131, 132), (), (), (133, 134, 146, 147, 148, 149), (), (), (),
-    (), (), (), (), (), (), (), (), (), (), (150, 161), (), (151, 152, 162, 163), (),
-    (153, 154, 164, 165, 172, 183), (), (173, 174, 184, 185), (155, 156, 166, 167),
-    (186, 187, 194, 205), (), (), (175, 176), (), (), (), (), (195,),
-    (157, 158, 168, 169, 196, 206, 207), (188, 189), (208, 209), (177, 178),
-    (159, 170, 190, 191, 197, 198), (160,), (179, 180, 192, 210, 211), (), (171, 193, 199, 200),
-    (181, 212, 213), (), (182, 201, 202, 214), (215,), (), (), (), (203,), (), (), (), (204,), (),
-    (), (216, 227), (217,), (218, 228, 229, 264, 265),
+    (84, 85), (), (64, 65, 69, 70, 113), (81, 82, 86, 87, 92, 93, 109, 110, 98, 114, 115, 136),
+    (284,), (88, 89, 66, 67, 116, 117), (143, 285), (), (71, 72, 111, 112, 94, 95, 121),
+    (73, 74, 137, 138), (99, 100), (), (96, 97), (101, 102), (122, 123), (128, 139, 140), (),
+    (103, 104), (), (124, 125), (), (118, 119, 129, 141, 142, 144, 145, 130),
+    (126, 127, 146, 147, 148, 149), (), (131, 132), (133, 134), (), (), (), (), (), (), (), (),
+    (), (150, 161), (), (151, 152, 162, 163), (), (153, 154, 164, 165, 172, 183), (),
+    (173, 174, 184, 185), (155, 156), (166, 167, 186, 187, 194, 205), (), (), (175, 176), (), (),
+    (), (), (195,), (196, 206, 207), (157, 158, 168, 169), (), (188, 189, 208, 209), (216, 227),
+    (177, 178, 217, 218, 228, 229), (159, 170, 190, 191, 197, 198), (210, 211), (160, 231),
+    (179, 180, 192), (), (199, 200, 212, 213, 220, 286), (171, 193), (), (181, 233),
+    (201, 202, 214), (), (182, 215), (), (222,), (235,), (), (203,), (236,), (), (238, 249),
+    (224, 237, 204, 239, 240, 250, 251, 287),
     (
-        219, 220, 238, 249, 230, 231, 239, 240, 250, 251, 221, 222, 232, 233, 223, 224, 234, 235,
-        241, 242, 225, 236, 243, 244, 237, 245, 246, 252, 253, 247, 254, 255, 226, 256, 257, 248,
-        258, 259,
+        260, 271, 225, 252, 255, 261, 241, 244, 262, 272, 273, 254, 257, 256, 243, 246, 258, 263,
+        266, 245, 277, 226, 274, 268, 259, 279, 265, 247, 276, 248, 267, 278, 269, 280, 270, 281,
     ),
 
 )
@@ -563,9 +566,10 @@
 
 
 class Scatter:
-    def __init__(self, me, buf, start, size, order, index, sems, landing, out, slot, credits):
+    def __init__(self, me, buf, targets, start, size, order, index, sems, landing, out, slot, credits):
         self.me, self.buf, self.order, self.index = me, buf, order, index
         self.rows = pl.ds(start, size)
+        self.lo, self.hi = targets
         self.sems = sems
         self.rc, self.rb, self.rz, self.ra = landing
         self.out = out
@@ -583,14 +587,17 @@
         me = self.me
         c = 1 - me.c if other else me.c
         if self.order == 0:
-            return self.buf.at[:, 1 - me.x if far else me.x, c, :, self.rows]
-        return self.buf.at[:, :, c, 1 - me.y if far else me.y, self.rows]
+            return self.buf.at[self.planes_z(), 1 - me.x if far else me.x, c, :, self.rows]
+        return self.buf.at[self.planes_z(), :, c, 1 - me.y if far else me.y, self.rows]
+
+    def planes_z(self):
+        return pl.ds(self.lo, self.hi - self.lo)
 
     def got_core(self, far, zz=None):
         half = 1 if far else 0
         if zz is None:
-            return self.rc.at[half, :, :, self.slot]
-        return self.rc.at[half, zz, :, self.slot]
+            return self.rc.at[half, 0 : self.hi - self.lo, :, self.slot]
+        return self.rc.at[half, zz - self.lo, :, self.slot]
 
     def core_copy(self, far):
         s, i = self.sems, self.index
@@ -607,13 +614,15 @@
         s, i = self.sems, self.index
         return remote(
             self.part(zz, True),
-            self.rb.at[zz],
+            self.rb.at[zz - self.lo],
             s.rb_s.at[i, zz],
             s.rb_r.at[i, zz],
             self.me.last(self.order),
         )
 
     def line_slot(self, zz, at, down):
+        if self.hi - self.lo == 1:
+            return zz - self.lo
         return zz if down else jnp.where(zz == at, NZ, zz)
 
     def line_copy(self, zz, down):
@@ -662,9 +671,12 @@
         if dist > 0:
             self.one_way(dist, False, act_up)
 
+    def aims(self, zz):
+        return (zz >= self.lo) & (zz < self.hi)
+
     def one_way(self, dist, down, act):
         zz = self.me.z - dist if down else self.me.z + dist
-        pl.when((zz >= 0) if down else (zz < NZ))(lambda: act(zz))
+        pl.when(self.aims(zz))(lambda: act(zz))
 
     def start(self):
         if self.after is not None:
@@ -686,7 +698,7 @@
 
     def keep(self):
         self.core_copy(False).wait_recv()
-        for zz in range(NZ):
+        for zz in range(self.lo, self.hi):
             ref = self.part(zz, False)
             got = self.got_core(False, zz)
             ref[...] = (ref[...].astype(F32) + got[...].astype(F32)).astype(BF16)
@@ -702,12 +714,13 @@
             self.last_copy(zz).wait_recv()
             ref = self.part(zz, False)
             outer = z < NZ - 1 if down else z > 0
-            total = ref[...].astype(F32) + self.rb[zz].astype(F32)
+            total = ref[...].astype(F32) + self.rb[zz - self.lo].astype(F32)
+            slot = self.line_slot(zz, z, True)
 
             @pl.when(outer)
             def _():
-                self.line_wait(zz)
-                ref[...] = (total + self.rz[zz].astype(F32)).astype(BF16)
+                self.line_wait(slot)
+                ref[...] = (total + self.rz[slot].astype(F32)).astype(BF16)
 
             @pl.when(jnp.logical_not(outer))
             def _():
@@ -726,48 +739,55 @@
         )
 
     def settle(self):
+        pl.when(self.aims(self.me.z))(self.settle_here)
+
+    def settle_here(self):
         z = self.me.z
         self.last_copy(z).wait_recv()
         far_ref, far = self.home(False)
         near_ref, near = self.home(True)
-        self.out[self.rows, :] = near_ref[...].astype(F32) + self.rb[z, near].astype(F32)
-        total = far_ref[...].astype(F32) + self.rb[z, far].astype(F32)
+        here = z - self.lo
+        above, below = self.line_slot(z, z, True), self.line_slot(z, z, False)
+        self.out[self.rows, :] = near_ref[...].astype(F32) + self.rb[here, near].astype(F32)
+        total = far_ref[...].astype(F32) + self.rb[here, far].astype(F32)
 
         @pl.when(z == 0)
         def _():
-            self.line_wait(z)
-            far_ref[...] = (total + self.rz[z, far].astype(F32)).astype(BF16)
-            self.out[self.rows, :] += self.rz[z, near].astype(F32)
+            self.line_wait(above)
+            far_ref[...] = (total + self.rz[above, far].astype(F32)).astype(BF16)
+            self.out[self.rows, :] += self.rz[above, near].astype(F32)
 
         @pl.when(z == NZ - 1)
         def _():
-            self.line_wait(NZ)
-            far_ref[...] = (total + self.rz[NZ, far].astype(F32)).astype(BF16)
-            self.out[self.rows, :] += self.rz[NZ, near].astype(F32)
+            self.line_wait(below)
+            far_ref[...] = (total + self.rz[below, far].astype(F32)).astype(BF16)
+            self.out[self.rows, :] += self.rz[below, near].astype(F32)
 
         @pl.when((z > 0) & (z < NZ - 1))
         def _():
-            self.line_wait(z)
-            self.line_wait(NZ)
+            self.line_wait(above)
+            self.line_wait(below)
             far_ref[...] = (
-                total + (self.rz[z, far].astype(F32) + self.rz[NZ, far].astype(F32))
+                total + (self.rz[above, far].astype(F32) + self.rz[below, far].astype(F32))
             ).astype(BF16)
-            self.out[self.rows, :] += self.rz[z, near].astype(F32) + self.rz[NZ, near].astype(
-                F32
-            )
+            self.out[self.rows, :] += self.rz[above, near].astype(F32) + self.rz[
+                below, near
+            ].astype(F32)
 
         self.first_copy().start()
 
     def finish(self):
-        self.first_copy().wait_recv()
-        self.out[self.rows, :] += self.ra[...].astype(F32)
+        @pl.when(self.aims(self.me.z))
+        def _():
+            self.first_copy().wait_recv()
+            self.out[self.rows, :] += self.ra[...].astype(F32)
 
     def drain(self):
         z = self.me.z
         self.core_copy(True).wait_send()
         self.core_copy(False).wait_send()
-        self.first_copy().wait_send()
-        for zz in range(NZ):
+        pl.when(self.aims(z))(lambda: self.first_copy().wait_send())
+        for zz in range(self.lo, self.hi):
             self.last_copy(zz).wait_send()
 
             @pl.when(zz < z)
@@ -818,44 +838,61 @@
     return value.reshape(-1, value.shape[-1])
 
 
-def attention_pair(queries, keys, values, bias):
-    first = lax.broadcasted_iota(jnp.int32, keys.shape, 1) < HEAD_DIM
-    zero = jnp.zeros((), BF16)
+def masked_halves(pair, other):
+    first = lax.broadcasted_iota(jnp.int32, pair.shape, 1) < HEAD_DIM
+    return jnp.where(first, pair, other), jnp.where(first, other, pair)
+
+
+def attention_pair(queries, keys, values, ask, bar):
     values_turned = values.T
+    queries_halves, keys_halves = masked_halves(queries, ask), masked_halves(keys, bar)
+    scores = [nt_dot(keys_halves[half], queries_halves[half]) for half in range(2)]
     contexts, totals = [], []
     for half in range(2):
-        keys_half = jnp.where(first if half == 0 else ~first, keys, zero)
-        scores = nt_dot(keys_half, queries) + bias
-        largest = jnp.max(scores, axis=0, keepdims=True)
-        exponent = jnp.exp(scores - largest)
+        largest = jnp.max(scores[half], axis=0, keepdims=True)
+        exponent = jnp.exp(scores[half] - largest)
         total = column_sum(exponent)
-        soft = (exponent * (1.0 / total)).astype(BF16)
-        contexts.append(
-            plain_dot(values_turned[half * HEAD_DIM : (half + 1) * HEAD_DIM, :], soft)
+        context = plain_dot(
+            values_turned[half * HEAD_DIM : (half + 1) * HEAD_DIM, :], exponent.astype(BF16)
         )
+        contexts.append(context * (1.0 / total))
         totals.append(largest + jnp.log(total))
     return jnp.concatenate(contexts, 0).T, jnp.concatenate(totals, 0)
 
 
-def attention_pair_back(queries, keys, values, grad_context, bias, log_total):
-    first = lax.broadcasted_iota(jnp.int32, keys.shape, 1) < HEAD_DIM
-    zero = jnp.zeros((), BF16)
+def attention_pair_back(queries, keys, values, grad_context, ask, bar, log_total):
     keys_turned = keys.T
+    zero = jnp.zeros_like(keys)
+    queries_asked, keys_barred = masked_halves(queries, ask), masked_halves(keys, bar)
+    queries_alone, values_alone = masked_halves(queries, zero), masked_halves(values, zero)
+    grad_alone = masked_halves(grad_context, zero)
+    width = ROW // 2
+    parts = [(slice(0, width), 0), (slice(0, width), 1), (slice(width, ROW), 0), (slice(width, ROW), 1)]
+
+    def scores_of(part):
+        span, half = part
+        return (
+            nt_dot(keys_barred[half], queries_asked[half][span]),
+            nt_dot(values_alone[half], grad_context[span]),
+        )
+
+    ahead = [scores_of(part) for part in parts[:2]]
     grad_queries = []
     grad_keys = grad_values = 0.0
-    for half in range(2):
-        mask = first if half == 0 else ~first
-        scores = nt_dot(jnp.where(mask, keys, zero), queries) + bias
-        soft = jnp.exp(scores - log_total[half : half + 1, :])
-        grad_soft = nt_dot(jnp.where(mask, values, zero), grad_context)
+    for place, (span, half) in enumerate(parts):
+        if place + 2 < len(parts):
+            ahead.append(scores_of(parts[place + 2]))
+        scores, grad_soft = ahead[place]
+        soft = jnp.exp(scores - log_total[half : half + 1, span])
         inner = column_sum(soft * grad_soft)
         grad_scores = (soft * (grad_soft - inner)).astype(BF16)
-        grad_values += plain_dot(soft.astype(BF16), jnp.where(mask, grad_context, zero))
-        grad_keys += plain_dot(grad_scores, jnp.where(mask, queries, zero))
+        grad_values += plain_dot(soft.astype(BF16), grad_alone[half][span])
+        grad_keys += plain_dot(grad_scores, queries_alone[half][span])
         grad_queries.append(
             plain_dot(keys_turned[half * HEAD_DIM : (half + 1) * HEAD_DIM, :], grad_scores)
         )
-    return jnp.concatenate(grad_queries, 0).T, grad_keys, grad_values
+    grad_queries = [jnp.concatenate(grad_queries[i : i + 2], 0).T for i in (0, 2)]
+    return jnp.concatenate(grad_queries, 0), grad_keys, grad_values
 
 
 def select_columns(permuted):
@@ -880,14 +917,14 @@
     b_r=(10, NZ),
     c_s=(10, NZ),
     c_r=(10, NZ),
-    rc_s=(10, 2),
-    rc_r=(10, 2),
-    rb_s=(10, NZ),
-    rb_r=(10, NZ),
-    rz_s=(10, NZ),
-    rz_r=(10, NZ + 1),
-    ra_s=(10,),
-    ra_r=(10,),
+    rc_s=(12, 2),
+    rc_r=(12, 2),
+    rb_s=(12, NZ),
+    rb_r=(12, NZ),
+    rz_s=(12, NZ),
+    rz_r=(12, NZ + 1),
+    ra_s=(12,),
+    ra_r=(12,),
     x_s=(4, 2),
     x_r=(4, 2),
     own=(4, 2),
@@ -895,15 +932,22 @@
     pool_r=(1,),
     stat_s=(5,),
     stat_r=(5,),
-    load=(3,),
+    load=(2,),
 )
 
 
-def pieces():
-    rest = PIECE - SPLIT_F
-    return [(0, SPLIT_F, rest), (PIECE, FULL_A - PIECE - rest, rest)] + [
-        (k * PIECE, SPLIT_F, rest) for k in range(PIECES)
+def gather_pieces():
+    return [(0, *GATHER_A[0]), (sum(GATHER_A[0]), *GATHER_A[1])] + [
+        (k * PIECE, SPLIT_F, PIECE - SPLIT_F) for k in range(PIECES)
     ]
+
+
+def scatter_pieces():
+    return (
+        gather_pieces()[2:]
+        + [(0, *SCATTER_O)]
+        + [(0, *SCATTER_A[0]), (sum(SCATTER_A[0]), *SCATTER_A[1])]
+    )
 
 
 def scratch():
@@ -921,7 +965,9 @@
         act=pltpu.VMEM((PIECES, TOKENS, BLOCK), BF16),
         slope=pltpu.VMEM((PIECES, TOKENS, BLOCK), BF16),
         acc=pltpu.VMEM((TOKENS, D), F32),
-        bias=pltpu.VMEM((OWN_ROWS, ROW, ROW), BF16),
+        ask=pltpu.VMEM((OWN_ROWS, ROW, 128), BF16),
+        bar=pltpu.VMEM((OWN_ROWS, ROW, 128), BF16),
+        rco=pltpu.VMEM((2, 1, 2, FULL_A, D), BF16),
         totals=pltpu.VMEM((OWN_ROWS * HEADS // 2, 2, ROW), F32),
         side=pltpu.VMEM((TOKENS, 128), F32),
         vec=pltpu.VMEM((16, 4 * D), F32),
@@ -931,6 +977,7 @@
         stat=pltpu.VMEM((8, 128), F32),
         stat_in=pltpu.VMEM((5, 8, 128), F32),
         pool_out=pltpu.VMEM((OWN_ROWS, 8, D), F32),
+        vector_pad=pltpu.VMEM((EXTRA, 128), F32),
         pool_in=pltpu.VMEM((OWN_ROWS, 8, D // 2), F32),
         credit=pltpu.SemaphoreType.REGULAR((2,)),
         free=pltpu.SemaphoreType.REGULAR,
@@ -939,11 +986,11 @@
 
 def landing_shapes():
     shapes = []
-    for _ in range(PIECES):
-        for size in (SPLIT_F, PIECE - SPLIT_F):
+    for sizes, targets in ((SIZES_F, NZ),) * PIECES + ((SCATTER_O, 1),):
+        for size in sizes:
             shapes += [
-                pltpu.VMEM((NZ, 2, size, D), BF16),
-                pltpu.VMEM((NZ + 1, 2, size, D), BF16),
+                pltpu.VMEM((targets, 2, size, D), BF16),
+                pltpu.VMEM((targets + 1 if targets > 1 else 1, 2, size, D), BF16),
                 pltpu.VMEM((size, D), BF16),
             ]
     return shapes
@@ -954,9 +1001,9 @@
     dy_in,
     wa_in,
     wf_in,
+    vector_in,
     ids,
     flags,
-    flag_column,
     out_y,
     out_dx,
     out_pooled,
@@ -979,6 +1026,12 @@
     def tile(i, size):
         return pl.ds(pl.multiple_of(i * size, size), size)
 
+    def row_ids(slot):
+        return ids[pl.ds(2 * y + slot, 1), :]
+
+    def row_flags(slot):
+        return flags[pl.ds(2 * y + slot, 1), :].astype(F32)
+
     def vector(row, quarter):
         return vec[row : row + 1, quarter * D : (quarter + 1) * D]
 
@@ -999,12 +1052,15 @@
     def _():
         pl.semaphore_signal(barrier, inc=1, device_id=me.at(z=z + 1), device_id_type=MESH)
 
-    load_a = pltpu.make_async_copy(wa_in, wa.at[z, x, c, y], sems.load.at[0])
-    load_f = pltpu.make_async_copy(wf_in, wf.at[z, x, c, y], sems.load.at[1])
-    load_s = pltpu.make_async_copy(flag_column, r.side, sems.load.at[2])
+    own_a, own_f = acc.at[0:SHARD_A], acc.at[SHARD_A : SHARD_A + SHARD_F]
+    load_a = pltpu.make_async_copy(wa_in, own_a, sems.load.at[0])
+    load_f = pltpu.make_async_copy(wf_in, own_f, sems.load.at[1])
     load_a.start()
     load_f.start()
-    load_s.start()
+    r.vector_pad[...] = jnp.zeros_like(r.vector_pad)
+    r.vector_pad[0:3, 0:SHARD_A] = vector_in[...]
+    wa[z, x, c, y, SHARD_A:FULL_A, :] = jnp.zeros((EXTRA, D), BF16)
+    wa[z, x, c, y, SHARD_A:FULL_A, 0:128] = r.vector_pad[...].astype(BF16)
 
     def row_copy(kind, src, dst, slot):
         return remote(
@@ -1060,28 +1116,34 @@
         return run
 
     gathers, scatters = [], []
-    for piece, (first_row, *sizes) in enumerate(pieces()):
+    for piece, (first_row, *sizes) in enumerate(gather_pieces()):
         for order in range(2):
             buf = wa if piece < 2 else wf
             start = first_row + order * sizes[0]
             gathers.append(Gather(me, buf, start, sizes[order], order, 2 * piece + order, sems))
-    for piece, (first_row, *sizes) in enumerate(pieces()[2:] + pieces()[:2]):
-        out = grad_f if piece < PIECES else grad_a
+    places = (0, 1, 2, 3, 0, 1)
+    for piece, (first_row, *sizes) in enumerate(scatter_pieces()):
+        lone = piece == PIECES
+        targets = (0, NZ) if piece < PIECES else (NZ - 1, NZ) if lone else (0, NZ - 1)
         for order in range(2):
-            size, i = sizes[order], 2 * (piece % PIECES) + order
+            size, i = sizes[order], 2 * places[piece] + order
             landing = (
-                r.rc,
+                r.rco if lone else r.rc,
                 landing_refs[3 * i].at[:, :, 0:size],
                 landing_refs[3 * i + 1].at[:, :, 0:size],
                 landing_refs[3 * i + 2].at[0:size],
             )
             credit = r.credit.at[order]
-            credits = (credit if piece > 0 else None, credit if piece < PIECES + 1 else None)
+            credits = (
+                None if lone or piece == 0 else credit,
+                None if lone or piece == len(places) - 1 else credit,
+            )
             slot = order * sizes[0]
             scatters.append(
                 Scatter(
-                    me, wf, first_row + slot, size, order, 2 * piece + order, sems, landing, out,
-                    slot, credits,
+                    me, wa if lone else wf, targets, first_row + slot, size, order,
+                    2 * piece + order, sems, landing, grad_f if piece < PIECES else grad_a, slot,
+                    credits,
                 )
             )
 
@@ -1095,22 +1157,25 @@
         jnp.int32
     )
     load_a.wait()
+    wa[z, x, c, y, 0:SHARD_A, :] = own_a[...].astype(BF16)
     pl.semaphore_wait(barrier, 4 + line_ends)
     plan.step()
     load_f.wait()
+    wf[z, x, c, y] = own_f[...].astype(BF16)
+    plan.step()
 
     gvec[...] = jnp.zeros_like(gvec)
     r.gbu[...] = jnp.zeros_like(r.gbu)
     stat[...] = jnp.zeros_like(stat)
     for slot in range(OWN_ROWS):
-        wide = jnp.broadcast_to(ids[slot].astype(F32), (128, ROW))
+        wide = jnp.broadcast_to(row_ids(slot).astype(F32), (128, ROW))
         tall = wide.T
-        for j in range(ROW // 128):
-            across = wide[:, j * 128 : (j + 1) * 128]
-            across = jnp.broadcast_to(across[0:1, :], (ROW, 128))
-            r.bias[slot, :, j * 128 : (j + 1) * 128] = jnp.where(
-                tall == across, 0.0, masked_score
-            ).astype(BF16)
+        flag_rows = jnp.broadcast_to(row_flags(slot), (128, ROW))
+        r.side[slot * ROW : (slot + 1) * ROW, :] = flag_rows.T
+        lane = lax.broadcasted_iota(jnp.int32, (ROW, 128), 1) % HEAD_DIM
+        same = tall == lane.astype(F32)
+        r.ask[slot] = jnp.where(same & (lane < SEGMENTS), 1.0, 0.0).astype(BF16)
+        r.bar[slot] = jnp.where(same | (lane >= SEGMENTS), 0.0, masked_score).astype(BF16)
         plan.step()
     ctx[...] = select_columns(False)
     fg[...] = select_columns(True)
@@ -1132,9 +1197,7 @@
         for k in range(PIECES):
             r.bu[k, :, q * 256 : (q + 1) * 256] = moved[:, k * 256 : (k + 1) * 256]
 
-    plan.step()
-    load_s.wait()
-    plan.step()
+    plan.step(2)
     for copy in x_owns:
         copy.wait()
     for copy in x_arrivals:
@@ -1172,7 +1235,8 @@
             qkv[rows, columns(pair, 0)],
             qkv[rows, columns(pair, 1)],
             qkv[rows, columns(pair, 2)],
-            r.bias[slot].astype(F32),
+            r.ask[slot],
+            r.bar[slot],
         )
         ctx[rows, columns(pair, 0)] = context.astype(BF16)
         r.totals[i] = total
@@ -1252,11 +1316,11 @@
 
     segments = lax.broadcasted_iota(jnp.int32, (SEGMENTS, ROW), 0)
     for slot in range(OWN_ROWS):
-        member = jnp.where(segments == ids[slot], 1.0, 0.0) * flags[slot]
+        member = jnp.where(segments == row_ids(slot), 1.0, 0.0) * row_flags(slot)
         sums = plain_dot(member.astype(BF16), dys[slot * ROW : (slot + 1) * ROW, :])
         counts = jnp.sum(member, axis=1, keepdims=True)
         r.pool_out[slot] = sums / jnp.maximum(counts, 1.0)
-        total = flags[slot]
+        total = row_flags(slot)
         stat[3:4, :] += sum(total[:, j * 128 : (j + 1) * 128] for j in range(ROW // 128))
 
     def half_lanes(which):
@@ -1346,16 +1410,43 @@
     stat_end(3)()
     stat_start(4)()
 
-    def attend_back_pair(i):
-        slot, pair = i // (HEADS // 2), i % (HEADS // 2)
+    def outer_back(i):
+        cols = pl.ds(pl.multiple_of(i * (D // 2), 128), D // 2)
+        value = tn_dot(fg[:, cols], ctx[...]).astype(BF16)
+        wa[3, i, :, :, 0:SHARD_A, :] = value.reshape(NC, NY, SHARD_A, D)
+
+    plan.loop(2, outer_back)
+
+    ctx[...] = select_columns(False)
+    fg[...] = select_columns(True)
+
+    def vectors_back(q, buf):
+        row = lax.broadcasted_iota(jnp.int32, (8, 1), 0)
+        plain = nt_dot(gvec[:, q * D : (q + 1) * D].astype(BF16), ctx[...])
+        piled = jnp.concatenate(
+            [r.gbu[k, :, q * 256 : (q + 1) * 256] for k in range(PIECES)], axis=1
+        )
+        moved = nt_dot(piled.astype(BF16), fg[...])
+        low = jnp.where(row == 1, jnp.broadcast_to(moved[0:1, :], plain.shape), plain)
+        low = jnp.concatenate([low, jnp.zeros_like(low)], axis=0).astype(BF16)
+        for j in range(8):
+            buf[q, j // 4, (j // 2) % 2, j % 2, SHARD_A:FULL_A, 0:128] = low[
+                :, j * 128 : (j + 1) * 128
+            ]
+
+    vectors_back(3, wa)
+    plan.step()
+
+    def attend_back_pair(slot, pair):
         rows = tile(slot, ROW)
         grads = attention_pair_back(
             qkv[rows, columns(pair, 0)],
             qkv[rows, columns(pair, 1)],
             qkv[rows, columns(pair, 2)],
             fn[rows, columns(pair, 0)],
-            r.bias[slot].astype(F32),
-            r.totals[i],
+            r.ask[slot],
+            r.bar[slot],
+            r.totals[slot * (HEADS // 2) + pair],
         )
         for j in range(3):
             low = grads[j].astype(BF16)
@@ -1365,71 +1456,53 @@
             if j != 1:
                 gvec[0:1, columns(pair, j // 2)] += column_sum(low.astype(F32))
 
-    plan.loop(OWN_ROWS * HEADS // 2, attend_back_pair)
-    stat_end(4)()
-    plan.step()
-    for one in scatters[:4]:
-        one.drain()
-
-    free = r.free
-    for where in (me.at(x=1 - x), me.at(y=1 - y)):
-        pl.semaphore_signal(free, inc=1, device_id=where, device_id_type=MESH)
-
-    @pl.when(z > 0)
-    def _():
-        pl.semaphore_signal(free, inc=1, device_id=me.at(z=z - 1), device_id_type=MESH)
-
-    @pl.when(z < NZ - 1)
-    def _():
-        pl.semaphore_signal(free, inc=1, device_id=me.at(z=z + 1), device_id_type=MESH)
-
-    for j in range(3):
-
-        def inner_back(i, j=j):
-            cols = pl.ds(pl.multiple_of(j * D + i * (D // 2), 128), D // 2)
-            value = tn_dot(qkv[:, cols], xs[...]).astype(BF16)
-            wf[j, i, :, :, 0:SHARD_A, :] = value.reshape(NC, NY, SHARD_A, D)
-
-        plan.loop(2, inner_back)
-
-    def outer_back(i):
-        cols = pl.ds(pl.multiple_of(i * (D // 2), 128), D // 2)
-        value = tn_dot(fg[:, cols], ctx[...]).astype(BF16)
-        wf[3, i, :, :, 0:SHARD_A, :] = value.reshape(NC, NY, SHARD_A, D)
-
-    plan.loop(2, outer_back)
-    pl.semaphore_wait(free, 2 + line_ends)
-
-    ctx[...] = select_columns(False)
-    fg[...] = select_columns(True)
-    row = lax.broadcasted_iota(jnp.int32, (8, 1), 0)
-    for q in range(4):
-        plain = nt_dot(gvec[:, q * D : (q + 1) * D].astype(BF16), ctx[...])
-        piled = jnp.concatenate(
-            [r.gbu[k, :, q * 256 : (q + 1) * 256] for k in range(PIECES)], axis=1
-        )
-        moved = nt_dot(piled.astype(BF16), fg[...])
-        low = jnp.where(row == 1, jnp.broadcast_to(moved[0:1, :], plain.shape), plain)
-        low = jnp.concatenate([low, jnp.zeros_like(low)], axis=0).astype(BF16)
-        for j in range(8):
-            wf[q, j // 4, (j // 2) % 2, j % 2, SHARD_A:FULL_A, 0:128] = low[
-                :, j * 128 : (j + 1) * 128
-            ]
-    plan.step()
-
-    def input_back(i):
-        rows = tile(i, 512)
+    def input_back(slot):
+        rows = pl.ds(slot * ROW, ROW)
         value = acc[rows, :]
         for j in range(3):
             value += plain_dot(
                 qkv[rows, j * D : (j + 1) * D], flatten(wa[j, :, :, :, 0:SHARD_A, :])
             )
         n1[rows, :] = value.astype(BF16)
-
-    plan.loop(2, input_back)
-    start_all(dx_owns)()
+        dx_owns[slot].start()
+
+    plan.loop(HEADS // 2, functools.partial(attend_back_pair, 0))
+    input_back(0)
     plan.step()
-
+    plan.loop(HEADS // 2, functools.partial(attend_back_pair, 1))
+    stat_end(4)()
+    plan.step()
+    for one in scatters[:4]:
+        one.drain()
+
+    free = r.free
+    for where in (me.at(x=1 - x), me.at(y=1 - y)):
+        pl.semaphore_signal(free, inc=1, device_id=where, device_id_type=MESH)
+
+    @pl.when(z > 0)
+    def _():
+        pl.semaphore_signal(free, inc=1, device_id=me.at(z=z - 1), device_id_type=MESH)
+
+    @pl.when(z < NZ - 1)
+    def _():
+        pl.semaphore_signal(free, inc=1, device_id=me.at(z=z + 1), device_id_type=MESH)
+
+    for j in range(3):
+
+        def inner_back(i, j=j):
+            cols = pl.ds(pl.multiple_of(j * D + i * (D // 2), 128), D // 2)
+            value = tn_dot(qkv[:, cols], xs[...]).astype(BF16)
+            wf[j, i, :, :, 0:SHARD_A, :] = value.reshape(NC, NY, SHARD_A, D)
+
+        plan.loop(2, inner_back)
+    for q in range(3):
+        vectors_back(q, wf)
+    pl.semaphore_wait(free, 2 + line_ends)
+    plan.step()
+    input_back(1)
+    plan.step(2)
+
+    assert plan.place == len(PLAN)
     for one in scatters[4:]:
         one.drain()
     pool_copy.wait()
@@ -1448,29 +1521,41 @@
             copy.wait_recv()
 
 
-def fused_call(inputs, output_grad, attention_low, feedforward_low, ids, flags, flag_column):
-    row_count, local_span, width = inputs.shape
-    any_space = pl.BlockSpec(memory_space=pl.ANY)
-    vmem = pl.BlockSpec(memory_space=pltpu.VMEM)
-    semaphores = [pltpu.SemaphoreType.DMA(shape) for shape in SEM_SHAPES.values()]
-    return pl.pallas_call(
-        fused_kernel,
-        out_shape=(
-            jax.ShapeDtypeStruct(inputs.shape, BF16),
-            jax.ShapeDtypeStruct(inputs.shape, BF16),
-            jax.ShapeDtypeStruct((row_count, SEGMENTS, D // NY), F32),
-            jax.ShapeDtypeStruct((8, 128), F32),
-            jax.ShapeDtypeStruct((FULL_A, D), F32),
-            jax.ShapeDtypeStruct((SHARD_F, D), F32),
-        ),
-        in_specs=[any_space] * 4 + [vmem] * 2 + [any_space],
-        out_specs=(any_space, any_space, vmem, vmem, vmem, vmem),
-        scratch_shapes=list(scratch().values()) + landing_shapes() + semaphores,
-        compiler_params=pltpu.CompilerParams(
-            collective_id=0, has_side_effects=True, vmem_limit_bytes=65_000 * 1024
-        ),
-        name="layer",
-    )(inputs, output_grad, attention_low, feedforward_low, ids, flags, flag_column)
+def finish_kernel(
+    y_in,
+    dx_in,
+    pooled_in,
+    stats,
+    grad_a,
+    grad_f,
+    *more,
+):
+    states, results, sems = more[:9], more[9:-1], more[-1]
+    out_y, out_dx, out_pooled, out_rms = results[:4]
+    copies = [
+        pltpu.make_async_copy(y_in, out_y, sems.at[0]),
+        pltpu.make_async_copy(dx_in, out_dx, sems.at[1]),
+    ]
+    for copy in copies:
+        copy.start()
+    out_pooled[...] = pooled_in[...]
+    totals = jnp.sum(stats[...], axis=1, keepdims=True)
+    rms = jnp.sqrt(totals[0:3] / D / totals[3:4])
+    for i in range(3):
+        out_rms[i] = rms[i, 0]
+    rates = (
+        (rate_attention, weight_decay),
+        (rate_feedforward, weight_decay),
+        (rate_vectors, 0.0),
+    )
+    gradients = (grad_a.at[0:SHARD_A], grad_f, grad_a.at[SHARD_A : SHARD_A + 3, 0:SHARD_A])
+    for i in range(3):
+        weight, first, second = states[3 * i : 3 * i + 3]
+        new = adamw_update(weight[...], gradients[i][...], first[...], second[...], *rates[i])
+        for ref, value in zip(results[4 + 4 * i : 8 + 4 * i], new):
+            ref[...] = value
+    for copy in copies:
+        copy.wait()
 
 
 def fused_shards(
@@ -1488,57 +1573,67 @@
     vector_first,
     vector_second,
 ):
-    seq = lax.axis_index("seq")
-    ids = lax.dynamic_slice_in_dim(segment_ids, seq * OWN_ROWS, OWN_ROWS, 0)
-    flags = lax.dynamic_slice_in_dim(token_flags, seq * OWN_ROWS, OWN_ROWS, 0).astype(F32)
-    flag_column = jnp.broadcast_to(flags.reshape(TOKENS, 1), (TOKENS, 128))
-    vector_rows = jnp.pad(layer_vectors, ((0, EXTRA - 3), (0, D - SHARD_A)))
-    attention_low = jnp.concatenate([attention_weights.T, vector_rows], axis=0).astype(BF16)
-    feedforward_low = feedforward_weights.T.astype(BF16)
-    output_rows, input_rows, pooled, stats, grad_a, grad_f = fused_call(
+    any_space = pl.BlockSpec(memory_space=pl.ANY)
+    vmem = pl.BlockSpec(memory_space=pltpu.VMEM)
+    smem = pl.BlockSpec(memory_space=pltpu.SMEM)
+    rows = jax.ShapeDtypeStruct(inputs.shape, BF16)
+    pooled = jax.ShapeDtypeStruct((inputs.shape[0], SEGMENTS, D // NY), F32)
+    semaphores = [pltpu.SemaphoreType.DMA(shape) for shape in SEM_SHAPES.values()]
+    passed = pl.pallas_call(
+        fused_kernel,
+        out_shape=(
+            rows,
+            rows,
+            pooled,
+            jax.ShapeDtypeStruct((8, 128), F32),
+            jax.ShapeDtypeStruct((FULL_A, D), F32),
+            jax.ShapeDtypeStruct((SHARD_F, D), F32),
+        ),
+        in_specs=[any_space] * 4 + [vmem] * 3,
+        out_specs=(any_space, any_space, vmem, vmem, vmem, vmem),
+        scratch_shapes=list(scratch().values()) + landing_shapes() + semaphores,
+        compiler_params=pltpu.CompilerParams(
+            collective_id=0, has_side_effects=True, vmem_limit_bytes=65_000 * 1024
+        ),
+        name="layer",
+    )(
         inputs,
         output_grad,
-        attention_low,
-        feedforward_low,
-        ids.reshape(OWN_ROWS, 1, ROW),
-        flags.reshape(OWN_ROWS, 1, ROW),
-        flag_column,
-    )
-    totals = jnp.sum(stats[0:4], axis=1)
-    stream_rms = jnp.sqrt(totals[0:3] / D / totals[3])
-    attention_new = adamw_update(
-        attention_weights,
-        grad_a[0:SHARD_A].T,
-        attention_first,
-        attention_second,
-        rate_attention,
-        weight_decay,
-    )
-    feedforward_new = adamw_update(
-        feedforward_weights,
-        grad_f.T,
-        feedforward_first,
-        feedforward_second,
-        rate_feedforward,
-        weight_decay,
-    )
-    vectors_new = adamw_update(
+        attention_weights.T,
+        feedforward_weights.T,
         layer_vectors,
-        grad_a[SHARD_A : SHARD_A + 3, 0:SHARD_A],
+        segment_ids,
+        token_flags,
+    )
+    states = (
+        attention_weights.T,
+        attention_first.T,
+        attention_second.T,
+        feedforward_weights.T,
+        feedforward_first.T,
+        feedforward_second.T,
+        layer_vectors,
         vector_first,
         vector_second,
-        rate_vectors,
-        0.0,
-    )
-    return (
-        output_rows,
-        input_rows,
-        pooled,
-        stream_rms,
-        *attention_new,
-        *feedforward_new,
-        *vectors_new,
-    )
+    )
+
+    def updated(shape):
+        wide = jax.ShapeDtypeStruct(shape, F32)
+        return (wide, wide, wide, jax.ShapeDtypeStruct(shape, BF16))
+
+    results = pl.pallas_call(
+        finish_kernel,
+        out_shape=(rows, rows, pooled, jax.ShapeDtypeStruct((3,), F32))
+        + updated((SHARD_A, D))
+        + updated((SHARD_F, D))
+        + updated(layer_vectors.shape),
+        in_specs=[vmem] * 15,
+        out_specs=(any_space, any_space, vmem, smem) + (vmem,) * 12,
+        scratch_shapes=[pltpu.SemaphoreType.DMA((2,))],
+        compiler_params=pltpu.CompilerParams(vmem_limit_bytes=65_000 * 1024),
+        name="finish",
+    )(*passed, *states)
+    return results[:4] + tuple(value.T for value in results[4:12]) + results[12:]
 
 
 def solution(mesh):

time: 238 us -> 216 us (0.908)
  other arithmetic: 13.3 us -> 0 us
  local copies, waits for them, and re-layouts: 6.55 us -> 0 us
    convert_element_type x5 -> x0, other arithmetic: 8.88 us -> none  [the longest x3 6.35 us: adamw_update(): return (weight_new, first_new, second_new, weight_new.astype(jnp.bfloat16))]
    unnamed x24 -> x0, local copies, waits for them, and re-layouts: 3.78 us -> none
    pallas_call x1 -> x2, Pallas kernels: 213 us -> 211 us  [the longest x1 205 us: fused_shards(): pl.pallas_call(fused_kernel, out_shape=(rows, rows, pooled, jax.ShapeDtyp...]
where the time goes in v1:
time: 216 us; the launch traced here: 212 us
  Pallas kernels  211 us (98%)
    pallas_call x1, Pallas kernels, fused_shards(): pl.pallas_call(fused_kernel, out_shape=(rows, rows, pooled, jax.ShapeDtyp...  205 us
    pallas_call x1, Pallas kernels, fused_shards(): pl.pallas_call(finish_kernel, out_shape=(rows, rows, pooled, jax.ShapeDty...  6.37 us

profile of v1, /device:TPU:0, one launch (start us, length us, event | category | flops | bytes accessed | tf_op | source)
XLA Modules:
  0.0 212.5 jit_solution(3421272612281826990)
XLA Ops:
  0.6 205.0 %layer.1 = (bf16[4,256,768]{2,1,0:T(8,128)(2,1)}, bf16[4,256,768]{2,1,0:T(8,128)(2,1)}, f32[4,8,384]{2,1,0:T(8,128)}, f32[8,128]{1,0:T(8,128)}, f32[112,768]{1,0:T(8,128)}, /*index=5*/f32[192,768]{1,0:T(8,128)}) custom-call(bf16[4,256,768]{2,1,0:T(8,128)(2,1)} %x_in.1, bf16[4,256,768]{2,1,0:T(8,128)(2,1)} %dy_in.1, f32[96,768]{1,0:T(8,128)} %bitcast.16, ...), custom_call_target="tpu_custom_call" | custom-call | tf_op jit(solution)/shard_map/layer/pallas_call | solution.py:1582
  205.6 6.4 %finish.1 = (bf16[4,256,768]{2,1,0:T(8,128)(2,1)}, bf16[4,256,768]{2,1,0:T(8,128)(2,1)}, f32[4,8,384]{2,1,0:T(8,128)}, f32[3]{0:T(128)}, f32[96,768]{1,0:T(8,128...) custom-call(bf16[4,256,768]{2,1,0:T(8,128)(2,1)} %get-tuple-element., ...), custom_call_target="tpu_custom_call" | custom-call | tf_op jit(solution)/shard_map/finish/pallas_call | solution.py:1624

commit v2 on v1

--- a/solution.py
+++ b/solution.py
@@ -986,7 +986,9 @@
 
 def landing_shapes():
     shapes = []
-    for sizes, targets in ((SIZES_F, NZ),) * PIECES + ((SCATTER_O, 1),):
+    shared = [tuple(map(max, SIZES_F, sizes)) for sizes in SCATTER_A]
+    places = [(sizes, NZ) for sizes in (*shared, SIZES_F)] + [(SCATTER_O, 1)]
+    for sizes, targets in places:
         for size in sizes:
             shapes += [
                 pltpu.VMEM((targets, 2, size, D), BF16),
@@ -1521,23 +1523,11 @@
             copy.wait_recv()
 
 
-def finish_kernel(
-    y_in,
-    dx_in,
-    pooled_in,
-    stats,
-    grad_a,
-    grad_f,
-    *more,
-):
-    states, results, sems = more[:9], more[9:-1], more[-1]
+def finish_kernel(y_in, dx_in, pooled_in, stats, grad_a, grad_f, grad_v, *more):
+    states, results = more[:9], more[9:]
     out_y, out_dx, out_pooled, out_rms = results[:4]
-    copies = [
-        pltpu.make_async_copy(y_in, out_y, sems.at[0]),
-        pltpu.make_async_copy(dx_in, out_dx, sems.at[1]),
-    ]
-    for copy in copies:
-        copy.start()
+    out_y[...] = y_in[...]
+    out_dx[...] = dx_in[...]
     out_pooled[...] = pooled_in[...]
     totals = jnp.sum(stats[...], axis=1, keepdims=True)
     rms = jnp.sqrt(totals[0:3] / D / totals[3:4])
@@ -1548,14 +1538,12 @@
         (rate_feedforward, weight_decay),
         (rate_vectors, 0.0),
     )
-    gradients = (grad_a.at[0:SHARD_A], grad_f, grad_a.at[SHARD_A : SHARD_A + 3, 0:SHARD_A])
+    gradients = (grad_a[...], grad_f[...], grad_v[0:3, 0:SHARD_A])
     for i in range(3):
         weight, first, second = states[3 * i : 3 * i + 3]
-        new = adamw_update(weight[...], gradients[i][...], first[...], second[...], *rates[i])
+        new = adamw_update(weight[...], gradients[i], first[...], second[...], *rates[i])
         for ref, value in zip(results[4 + 4 * i : 8 + 4 * i], new):
             ref[...] = value
-    for copy in copies:
-        copy.wait()
 
 
 def fused_shards(
@@ -1621,18 +1609,35 @@
         wide = jax.ShapeDtypeStruct(shape, F32)
         return (wide, wide, wide, jax.ShapeDtypeStruct(shape, BF16))
 
+    steps = 2
+
+    def part(shape):
+        return pl.BlockSpec((shape[0] // steps, *shape[1:]), lambda i: (i,) + (0,) * (len(shape) - 1))
+
+    def whole(shape):
+        return pl.BlockSpec(shape, lambda i: (0,) * len(shape))
+
+    table_a, table_f, table_v = (SHARD_A, D), (SHARD_F, D), layer_vectors.shape
     results = pl.pallas_call(
         finish_kernel,
+        grid=(steps,),
         out_shape=(rows, rows, pooled, jax.ShapeDtypeStruct((3,), F32))
-        + updated((SHARD_A, D))
-        + updated((SHARD_F, D))
-        + updated(layer_vectors.shape),
-        in_specs=[vmem] * 15,
-        out_specs=(any_space, any_space, vmem, smem) + (vmem,) * 12,
-        scratch_shapes=[pltpu.SemaphoreType.DMA((2,))],
+        + updated(table_a)
+        + updated(table_f)
+        + updated(table_v),
+        in_specs=[part(rows.shape), part(rows.shape), part(pooled.shape), whole((8, 128))]
+        + [part(table_a), part(table_f), pl.BlockSpec((EXTRA, D), lambda i: (SHARD_A // EXTRA, 0))]
+        + [part(table_a)] * 3
+        + [part(table_f)] * 3
+        + [whole(table_v)] * 3,
+        out_specs=[part(rows.shape), part(rows.shape), part(pooled.shape), smem]
+        + [part(table_a)] * 4
+        + [part(table_f)] * 4
+        + [whole(table_v)] * 4,
         compiler_params=pltpu.CompilerParams(vmem_limit_bytes=65_000 * 1024),
         name="finish",
-    )(*passed, *states)
+    )(*passed, passed[4], *states)
+    results = tuple(results)
     return results[:4] + tuple(value.T for value in results[4:12]) + results[12:]
 
 

time: 216 us -> 214 us (level)
  no operation moved by 1% of the time
where the time goes in v2:
time: 214 us; the launch traced here: 211 us
  Pallas kernels  210 us (98%)
    pallas_call x1, Pallas kernels, fused_shards(): pl.pallas_call(fused_kernel, out_shape=(rows, rows, pooled, jax.ShapeDtyp...  205 us
    pallas_call x1, Pallas kernels, fused_shards(): pl.pallas_call(finish_kernel, grid=(steps,), out_shape=(rows, rows, poole...  4.91 us

profile of v2, /device:TPU:0, one launch (start us, length us, event | category | flops | bytes accessed | tf_op | source)
XLA Modules:
  0.0 210.7 jit_solution(13339297124238084784)
XLA Ops:
  0.6 204.9 %layer.1 = (bf16[4,256,768]{2,1,0:T(8,128)(2,1)}, bf16[4,256,768]{2,1,0:T(8,128)(2,1)}, f32[4,8,384]{2,1,0:T(8,128)}, f32[8,128]{1,0:T(8,128)}, f32[112,768]{1,0:T(8,128)}, /*index=5*/f32[192,768]{1,0:T(8,128)}) custom-call(bf16[4,256,768]{2,1,0:T(8,128)(2,1)} %x_in.1, bf16[4,256,768]{2,1,0:T(8,128)(2,1)} %dy_in.1, f32[96,768]{1,0:T(8,128)} %bitcast.16, ...), custom_call_target="tpu_custom_call" | custom-call | tf_op jit(solution)/shard_map/layer/pallas_call | solution.py:1570
  205.5 4.9 %finish.1 = (bf16[4,256,768]{2,1,0:T(8,128)(2,1)}, bf16[4,256,768]{2,1,0:T(8,128)(2,1)}, f32[4,8,384]{2,1,0:T(8,128)}, f32[3]{0:T(128)}, f32[96,768]{1,0:T(8,128...) custom-call(bf16[4,256,768]{2,1,0:T(8,128)(2,1)} %get-tuple-element., ...), custom_call_target="tpu_custom_call" | custom-call | tf_op jit(solution)/shard_map/finish/pallas_call | solution.py:1621

commit v3 on v2

--- a/solution.py
+++ b/solution.py
@@ -1297,7 +1297,7 @@
         one.drain()
 
     def second(i):
-        rows = tile(i, 128)
+        rows = tile(i, 256)
         feed_out = acc[rows, :] + vector(0, 3)
         stat[2:3, :] += lane_sums(feed_out * feed_out * r.side[rows, 1:2])
         normed, inverse = normalize(fn[rows, :].astype(F32) + feed_out)
@@ -1311,7 +1311,7 @@
         fg[rows, :] = low
         gvec[0:1, 3 * D :] += column_sum(low.astype(F32))
 
-    repeat(TOKENS // 128, second)
+    repeat(TOKENS // 256, second)
     plan.step()
 
     start_all(out_sends + out_owns)()

time: 214 us -> 214 us (level)
  no operation moved by 1% of the time
where the time goes in v3:
time: 214 us; the launch traced here: 211 us
  Pallas kernels  210 us (98%)
    pallas_call x1, Pallas kernels, fused_shards(): pl.pallas_call(fused_kernel, out_shape=(rows, rows, pooled, jax.ShapeDtyp...  205 us
    pallas_call x1, Pallas kernels, fused_shards(): pl.pallas_call(finish_kernel, grid=(steps,), out_shape=(rows, rows, poole...  4.91 us

profile of v3, /device:TPU:0, one launch (start us, length us, event | category | flops | bytes accessed | tf_op | source)
XLA Modules:
  0.0 210.7 jit_solution(17578927156132862037)
XLA Ops:
  0.6 204.7 %layer.1 = (bf16[4,256,768]{2,1,0:T(8,128)(2,1)}, bf16[4,256,768]{2,1,0:T(8,128)(2,1)}, f32[4,8,384]{2,1,0:T(8,128)}, f32[8,128]{1,0:T(8,128)}, f32[112,768]{1,0:T(8,128)}, /*index=5*/f32[192,768]{1,0:T(8,128)}) custom-call(bf16[4,256,768]{2,1,0:T(8,128)(2,1)} %x_in.1, bf16[4,256,768]{2,1,0:T(8,128)(2,1)} %dy_in.1, f32[96,768]{1,0:T(8,128)} %bitcast.16, ...), custom_call_target="tpu_custom_call" | custom-call | tf_op jit(solution)/shard_map/layer/pallas_call | solution.py:1570
  205.3 4.9 %finish.1 = (bf16[4,256,768]{2,1,0:T(8,128)(2,1)}, bf16[4,256,768]{2,1,0:T(8,128)(2,1)}, f32[4,8,384]{2,1,0:T(8,128)}, f32[3]{0:T(128)}, f32[96,768]{1,0:T(8,128...) custom-call(bf16[4,256,768]{2,1,0:T(8,128)(2,1)} %get-tuple-element., ...), custom_call_target="tpu_custom_call" | custom-call | tf_op jit(solution)/shard_map/finish/pallas_call | solution.py:1621
